TPU v7x, 32 devices: a whole 2x2x4 slice. The times are simulated.
32 devices in a mesh: wide: 8 (over z, y), narrow: 4 (over x, core).
Axes of the slice: x: 2, y: 2, z: 4, core: 2. Of those that a mesh axis runs over, the one named last changes fastest.
Arguments:
- target_slot: int32 [1024], replicated, may hold values from 0 to 1023, as said below
- fields: bfloat16 [1024, 8, 4096], P(('wide', 'narrow')), as said below
Outputs:
- migrated: bfloat16 [1024, 8, 4096], P(('wide', 'narrow'))
- pressure: float32 [64, 512, 128], P('narrow', 'wide')
Inputs may be any that keep to these rules, and one draw needn't show every extreme that they name: `target_slot`: A permutation of the patches. Owner w * 4 + n holds patches w * 4 + n times 32 onward, old and new. From one owner to any owner go at most 2 patches, and exactly 2 for some pairs in every draw; every owner receives exactly 32 patches. `fields`: fields 0, 1, 2 are velocity components along the three dimensions, field 3 is the density, between 0.6 and 8.1; the others are carried quantities.
All inputs are finite; a program needn't handle non-finite values.
Results may differ from a plain program's by a relative error of at most 0.0014.
Values may be sent and summed in bfloat16 or wider, within the bound.
A program may use at most 128 MiB of HBM per device.

v0:
```python
import functools

import jax
import jax.numpy as jnp
from jax import lax
from jax.experimental import pallas as pl
from jax.experimental.pallas import tpu as pltpu
from jax.sharding import PartitionSpec as P

PATCH = 16
BYP = 4
BZP = 8
LEVELS = 3
BOTTOM = 16
DAMPING = 0.8
KEEP = 1.0 - DAMPING
SOLVED = 4
CAPACITY = 2
X0 = PATCH
Y0 = PATCH * BYP
Z = PATCH * BZP
PAD = 8
MESH = pl.DeviceIdType.MESH
STRIDE = 15
SHARES = (4, 3, 3) + (2,) * 10 + (1, 0)
VMEM_LIMIT = 60 * 1024 * 1024


def dims(level):
    return X0 >> level, Y0 >> level


def pack_kernel(index_ref, fields_ref, solved_ref, carried_ref):
    def one(slot, carry):
        patch = fields_ref[index_ref[slot]]
        solved_ref[slot] = patch[:SOLVED]
        carried_ref[slot] = patch[SOLVED:]
        return carry

    lax.fori_loop(0, solved_ref.shape[0], one, 0, unroll=8)


def merge_kernel(index_ref, solved_ref, carried_ref, out_ref):
    def one(patch, carry):
        row = index_ref[patch]
        out_ref[patch, :SOLVED] = solved_ref[row]
        out_ref[patch, SOLVED:] = carried_ref[row]
        return carry

    lax.fori_loop(0, out_ref.shape[0], one, 0, unroll=8)


def solve_kernel(
    n_wide,
    n_narrow,
    index_ref,
    solved_ref,
    carried_ref,
    out_ref,
    arrived_ref,
    moved_ref,
    turn,
    tmp,
    grid_u,
    grid_v,
    grid_w,
    grid_r,
    field_sent,
    field_got,
    iterates,
    sent_rows,
    got_rows,
    face_x,
    face_yl,
    face_yh,
    face_zl,
    face_zh,
    diag,
    weight,
    source,
    answer,
    gather_faces,
    gather_source,
    coef,
    send_sem,
    recv_sem,
    gsend_sem,
    grecv_sem,
    carry_send_sem,
    carry_recv_sem,
    own_sem,
    solved_send_sem,
    solved_recv_sem,
):
    wide = lax.axis_index("wide")
    narrow = lax.axis_index("narrow")
    has = {
        "xl": narrow > 0,
        "xh": narrow < n_narrow - 1,
        "yl": wide > 0,
        "yh": wide < n_wide - 1,
    }
    peer = {
        "xl": (wide, narrow - 1),
        "xh": (wide, narrow + 1),
        "yl": (wide - 1, narrow),
        "yh": (wide + 1, narrow),
    }
    order = ("xl", "xh", "yl", "yh")
    others = [(wide, lax.rem(narrow + d, n_narrow)) for d in range(1, n_narrow)]

    barrier = pltpu.get_barrier_semaphore()
    owners = n_wide * n_narrow
    me = wide * n_narrow + narrow

    def owner_at(distance):
        owner = lax.rem(me + distance, owners)
        return owner, (owner // n_narrow, lax.rem(owner, n_narrow))

    def greet(d, carry):
        _, device = owner_at(d)
        pl.semaphore_signal(barrier, inc=1, device_id=device, device_id_type=MESH)
        return carry

    lax.fori_loop(1, owners, greet, 0)
    pl.semaphore_wait(barrier, owners - 1)

    def block(owner):
        return pl.ds(owner * CAPACITY, CAPACITY)

    def carry_copy(k):
        d = lax.rem(k * STRIDE, owners)
        owner, device = owner_at(d)
        return pltpu.make_async_remote_copy(
            src_ref=carried_ref.at[block(owner)],
            dst_ref=moved_ref.at[block(me)],
            send_sem=carry_send_sem.at[k],
            recv_sem=carry_recv_sem.at[k],
            device_id=device,
            device_id_type=MESH,
        )

    def carry_landing(k):
        d = lax.rem(k * STRIDE, owners)
        _, device = owner_at(d)
        came, _ = owner_at(owners - d)
        return pltpu.make_async_remote_copy(
            src_ref=carried_ref.at[block(me)],
            dst_ref=moved_ref.at[block(came)],
            send_sem=carry_send_sem.at[k],
            recv_sem=carry_recv_sem.at[k],
            device_id=device,
            device_id_type=MESH,
        )

    def solved_copy(k):
        d = lax.rem(k * STRIDE, owners)
        owner, device = owner_at(d)
        return pltpu.make_async_remote_copy(
            src_ref=solved_ref.at[block(owner)],
            dst_ref=arrived_ref.at[block(me)],
            send_sem=solved_send_sem.at[k],
            recv_sem=solved_recv_sem.at[k],
            device_id=device,
            device_id_type=MESH,
        )

    def solved_landing(k):
        d = lax.rem(k * STRIDE, owners)
        _, device = owner_at(d)
        came, _ = owner_at(owners - d)
        return pltpu.make_async_remote_copy(
            src_ref=solved_ref.at[block(me)],
            dst_ref=arrived_ref.at[block(came)],
            send_sem=solved_send_sem.at[k],
            recv_sem=solved_recv_sem.at[k],
            device_id=device,
            device_id_type=MESH,
        )

    def solved_begin(k, carry):
        solved_copy(k).start()
        return carry

    def solved_arrive(k, carry):
        solved_landing(k).wait_recv()
        return carry

    def solved_end(k, carry):
        solved_copy(k).wait_send()
        return carry

    lax.fori_loop(1, owners, solved_begin, 0)
    own_solved = pltpu.make_async_copy(
        solved_ref.at[block(me)], arrived_ref.at[block(me)], own_sem.at[1]
    )
    own_solved.start()
    own_copy = pltpu.make_async_copy(
        carried_ref.at[block(me)], moved_ref.at[block(me)], own_sem.at[0]
    )
    own_copy.start()
    shares = SHARES
    bounds = [
        1 + (owners - 1) * sum(shares[:k]) // sum(shares) for k in range(len(shares) + 1)
    ]
    pushed = []

    def push():
        turn_now = len(pushed)
        pushed.append(turn_now)

        def begin(k, carry):
            carry_copy(k).start()
            return carry

        lax.fori_loop(bounds[turn_now], bounds[turn_now + 1], begin, 0)

    own_solved.wait()
    lax.fori_loop(1, owners, solved_arrive, 0)
    push()

    lane = lax.broadcasted_iota(jnp.int32, (8, Z), 1)
    block_lane = lane // PATCH

    lower_bits = [(block_lane // s) % 2 == 1 for s in (1, 2, 4)]

    def to_grid(step, carry):
        b = step // X0
        i = step % X0
        at = pl.multiple_of(i * 2 * Z, 2 * Z)
        rows = []
        for c in range(BZP):
            both = arrived_ref[index_ref[b * BZP + c], :, pl.ds(at, 2 * Z)].astype(
                jnp.float32
            )
            rows.append(jnp.concatenate([both[:, :Z], both[:, Z:]], axis=0))
        for bit, s in zip(lower_bits, (1, 2, 4)):
            new = list(rows)
            for c in range(BZP):
                if c & s == 0:
                    low, high = rows[c], rows[c + s]
                    new[c] = jnp.where(bit, pltpu.roll(high, PATCH * s, 1), low)
                    new[c + s] = jnp.where(bit, high, pltpu.roll(low, Z - PATCH * s, 1))
            rows = new
        for j in range(8):
            turn[8 * j : 8 * j + 8, :] = rows[j]
        for half in range(2):
            y = pl.multiple_of(b * PATCH + half * 8, 8)
            for f, ref in enumerate((grid_u, grid_v, grid_w, grid_r)):
                values = turn[pl.ds(half * SOLVED + f, 8, stride=8), :]
                if f == 2:
                    ref[i, pl.ds(y, 8), :] = values
                else:
                    ref[i + 1, pl.ds(PAD + y, 8), :] = values
        return carry

    lax.fori_loop(0, BYP * X0, to_grid, 0, unroll=8)

    def exchange(padded, X, Y, sent, got, slot, sides):
        mid = pl.ds(PAD, Y)
        ends = {
            "xl": (lambda: padded.at[1, mid], lambda: padded.at[X + 1, mid]),
            "xh": (lambda: padded.at[X, mid], lambda: padded.at[0, mid]),
            "yl": (lambda: sent.at[0], lambda: got.at[1]),
            "yh": (lambda: sent.at[1], lambda: got.at[0]),
        }
        back = {"xl": "xh", "xh": "xl", "yl": "yh", "yh": "yl"}

        def copy(side):
            src, dst = ends[side]
            return pltpu.make_async_remote_copy(
                src_ref=src(),
                dst_ref=dst(),
                send_sem=send_sem.at[slot, order.index(side)],
                recv_sem=recv_sem.at[slot, order.index(back[side])],
                device_id=peer[side],
                device_id_type=MESH,
            )

        def landing(side):
            src, dst = ends[back[side]]
            return pltpu.make_async_remote_copy(
                src_ref=src(),
                dst_ref=dst(),
                send_sem=send_sem.at[slot, order.index(side)],
                recv_sem=recv_sem.at[slot, order.index(side)],
                device_id=peer[side],
                device_id_type=MESH,
            )

        def start():
            for side in sides:

                @pl.when(has[side])
                def _():
                    copy(side).start()

        def finish():
            for side in sides:

                @pl.when(has[side])
                def _():
                    landing(side).wait_recv()

                @pl.when(jnp.logical_not(has[side]))
                def _():
                    if side == "xl":
                        padded[0, PAD : PAD + Y, :] = jnp.zeros((Y, Z), jnp.float32)
                    elif side == "xh":
                        padded[X + 1, PAD : PAD + Y, :] = jnp.zeros((Y, Z), jnp.float32)
                    elif side == "yl":
                        got[0] = jnp.zeros((X, Z), jnp.float32)
                    else:
                        got[1] = jnp.zeros((X, Z), jnp.float32)

            if "yl" in sides:

                for x in range(X):
                    padded[x + 1, PAD - 1 : PAD, :] = got[0, x : x + 1, :]
                    padded[x + 1, PAD + Y : PAD + Y + 1, :] = got[1, x : x + 1, :]

        def drain():
            for side in sides:

                @pl.when(has[side])
                def _():
                    copy(side).wait_send()

        return start, finish, drain

    drains = []

    for k, ref in ((0, grid_v), (1, grid_r)):
        for x in range(X0):
            field_sent[k, 0, x : x + 1, :] = ref[x + 1, PAD : PAD + 1, :]
            field_sent[k, 1, x : x + 1, :] = ref[x + 1, PAD + Y0 - 1 : PAD + Y0, :]
    field_moves = [
        exchange(grid_r, X0, Y0, field_sent.at[1], field_got.at[1], 0, order),
        exchange(grid_u, X0, Y0, None, None, 1, ("xl", "xh")),
        exchange(grid_v, X0, Y0, field_sent.at[0], field_got.at[0], 2, ("yl", "yh")),
    ]
    for start, finish, drain in field_moves:
        start()
        drains.append(drain)
    push()
    for start, finish, drain in field_moves:
        finish()

    def z_low(values, step):
        rolled = pltpu.roll(values, step, 1)
        at = lax.broadcasted_iota(jnp.int32, values.shape, 1)
        return jnp.where(at < step, 0.0, rolled)

    def z_high(values, step):
        rolled = pltpu.roll(values, Z - step, 1)
        at = lax.broadcasted_iota(jnp.int32, values.shape, 1)
        return jnp.where(at >= Z - step, 0.0, rolled)

    mid0 = pl.ds(PAD, Y0)

    def first(x, carry):
        here = grid_r[x + 1, mid0, :]
        fxl = 2.0 / (grid_r[x, mid0, :] + here)
        fxh = 2.0 / (here + grid_r[x + 2, mid0, :])
        fyl = 2.0 / (grid_r[x + 1, PAD - 1 : PAD - 1 + Y0, :] + here)
        fyh = 2.0 / (grid_r[x + 1, PAD + 1 : PAD + 1 + Y0, :] + here)
        fzl = 2.0 / (z_low(here, 1) + here)
        fzh = 2.0 / (z_high(here, 1) + here)
        face_x[0][x] = fxl
        face_x[0][x + 1] = fxh
        face_yl[0][x] = fyl
        face_yh[0][x] = fyh
        face_zl[0][x] = fzl
        face_zh[0][x] = fzh
        total = ((fxl + fxh) + (fyl + fyh)) + (fzl + fzh)
        diag[0][x] = total
        weight[0][x] = DAMPING / total
        w = grid_w[x]
        du = grid_u[x + 2, mid0, :] - grid_u[x, mid0, :]
        dv = (
            grid_v[x + 1, PAD + 1 : PAD + 1 + Y0, :]
            - grid_v[x + 1, PAD - 1 : PAD - 1 + Y0, :]
        )
        source[0][x] = -0.5 * ((du + dv) + (z_high(w, 1) - z_low(w, 1)))
        return carry

    lax.fori_loop(0, X0, first, 0, unroll=4)

    def z_bit(shape, level):
        at = lax.broadcasted_iota(jnp.int32, shape, 1)
        return (at // (1 << level)) % 2 == 1

    def z_pair(values, level):
        step = 1 << level
        other = jnp.where(
            z_bit(values.shape, level),
            pltpu.roll(values, step, 1),
            pltpu.roll(values, Z - step, 1),
        )
        return values + other

    def z_even(values, level):
        step = 1 << level
        return jnp.where(
            z_bit(values.shape, level), pltpu.roll(values, step, 1), values
        )

    def z_odd(values, level):
        step = 1 << level
        return jnp.where(
            z_bit(values.shape, level), values, pltpu.roll(values, Z - step, 1)
        )

    for level in range(LEVELS):
        X, Y = dims(level + 1)
        even, odd = pl.ds(0, Y, stride=2), pl.ds(1, Y, stride=2)
        last = level + 1 == LEVELS

        def coarse_x(x, level=level, even=even, odd=odd):
            fx = face_x[level]
            return 0.25 * z_pair(fx[2 * x, even, :] + fx[2 * x, odd, :], level)

        def coarse_rest(x, level=level, even=even, odd=odd):
            yl, yh = face_yl[level], face_yh[level]
            zl, zh = face_zl[level], face_zh[level]
            fyl = 0.25 * z_pair(yl[2 * x, even, :] + yl[2 * x + 1, even, :], level)
            fyh = 0.25 * z_pair(yh[2 * x, odd, :] + yh[2 * x + 1, odd, :], level)
            four_l = (zl[2 * x, even, :] + zl[2 * x, odd, :]) + (
                zl[2 * x + 1, even, :] + zl[2 * x + 1, odd, :]
            )
            four_h = (zh[2 * x, even, :] + zh[2 * x, odd, :]) + (
                zh[2 * x + 1, even, :] + zh[2 * x + 1, odd, :]
            )
            return fyl, fyh, z_even(0.25 * four_l, level), z_odd(0.25 * four_h, level)

        if last:
            for x in range(X + 1):
                gather_faces[narrow, x] = coarse_x(x)
            for x in range(X):
                for k, face in enumerate(coarse_rest(x)):
                    gather_faces[narrow, X + 1 + k * X + x] = face
        else:

            def planes(x, carry, level=level, rest=coarse_rest, cx=coarse_x):
                fxl, fxh = cx(x), cx(x + 1)
                fyl, fyh, fzl, fzh = rest(x)
                face_x[level + 1][x] = fxl
                face_x[level + 1][x + 1] = fxh
                face_yl[level + 1][x] = fyl
                face_yh[level + 1][x] = fyh
                face_zl[level + 1][x] = fzl
                face_zh[level + 1][x] = fzh
                total = ((fxl + fxh) + (fyl + fyh)) + (fzl + fzh)
                diag[level + 1][x] = total
                weight[level + 1][x] = DAMPING / total
                return carry

            lax.fori_loop(0, X, planes, 0, unroll=4)

    def gather(ref, which):
        def copy(d):
            return pltpu.make_async_remote_copy(
                src_ref=ref.at[narrow],
                dst_ref=ref.at[narrow],
                send_sem=gsend_sem.at[which, d - 1],
                recv_sem=grecv_sem.at[which, d - 1],
                device_id=others[d - 1],
                device_id_type=MESH,
            )

        def landing(d):
            came = lax.rem(narrow + n_narrow - d, n_narrow)
            return pltpu.make_async_remote_copy(
                src_ref=ref.at[narrow],
                dst_ref=ref.at[came],
                send_sem=gsend_sem.at[which, d - 1],
                recv_sem=grecv_sem.at[which, d - 1],
                device_id=others[d - 1],
                device_id_type=MESH,
            )

        def start():
            for d in range(1, n_narrow):
                copy(d).start()

        def finish():
            for d in range(1, n_narrow):
                landing(d).wait_recv()

        def drain():
            for d in range(1, n_narrow):
                copy(d).wait_send()

        return start, finish, drain

    face_start, face_finish, face_drain = gather(gather_faces, 0)
    source_start, source_finish, source_drain = gather(gather_source, 1)
    face_start()

    def neighbour_sum(level, e, x):
        _, Y = dims(level)
        p = iterates[level]
        step = 1 << level
        mid = pl.ds(PAD, Y)
        here = p[e, x + 1, mid, :]
        total = (
            face_x[level][x] * p[e, x, mid, :]
            + face_x[level][x + 1] * p[e, x + 2, mid, :]
        )
        total += face_yl[level][x] * p[e, x + 1, PAD - 1 : PAD - 1 + Y, :]
        total += face_yh[level][x] * p[e, x + 1, PAD + 1 : PAD + 1 + Y, :]
        total += face_zl[level][x] * z_low(here, step)
        total += face_zh[level][x] * z_high(here, step)
        return here, total

    def sweep(level, e, x):
        here, total = neighbour_sum(level, e, x)
        return KEEP * here + weight[level][x] * (source[level][x] + total)

    def produce(level, e, values_of):
        X, Y = dims(level)
        p = iterates[level]

        def plane(x, carry):
            v = values_of(x)
            p[e, x + 1, PAD : PAD + Y, :] = v
            sent_rows[level][e, 0, pl.ds(x, 1), :] = v[:1]
            sent_rows[level][e, 1, pl.ds(x, 1), :] = v[Y - 1 :]
            return carry

        lax.fori_loop(0, X, plane, 0, unroll=4)
        start, finish, drain = exchange(
            p.at[e],
            X,
            Y,
            sent_rows[level].at[e],
            got_rows[level].at[e],
            3 + 4 * level + e,
            order,
        )
        start()
        drains.append(drain)
        push()
        finish()

    for level in range(LEVELS):
        X, Y = dims(level)
        produce(level, 0, lambda x, level=level: weight[level][x] * source[level][x])
        produce(level, 1, lambda x, level=level: sweep(level, 0, x))

        def restrict(x, carry, level=level, Y=Y):
            both = None
            for k in range(2):
                here, total = neighbour_sum(level, 1, 2 * x + k)
                left = (source[level][2 * x + k] - diag[level][2 * x + k] * here) + total
                both = left if both is None else both + left
            tmp[:Y, :] = both
            half = Y // 2
            summed = (
                tmp[pl.ds(0, half, stride=2), :] + tmp[pl.ds(1, half, stride=2), :]
            )
            summed = 0.5 * z_pair(summed, level)
            if level + 1 == LEVELS:
                gather_source[narrow, x] = summed
            else:
                source[level + 1][x] = summed
            return carry

        if level + 1 == LEVELS:
            for x in range(X // 2):
                restrict(x, 0)
        else:
            lax.fori_loop(0, X // 2, restrict, 0, unroll=4)

    source_start()
    push()
    face_finish()
    source_finish()
    X, Y = dims(LEVELS)
    step = 1 << LEVELS
    row = lax.broadcasted_iota(jnp.int32, (Y, Z), 0)
    col = lax.broadcasted_iota(jnp.int32, (Y, Z), 1)
    for n in range(n_narrow):
        for x in range(X):
            fxl, fxh = gather_faces[n, x], gather_faces[n, x + 1]
            fyl, fyh, fzl, fzh = (gather_faces[n, X + 1 + k * X + x] for k in range(4))
            total = ((fxl + fxh) + (fyl + fyh)) + (fzl + fzh)
            w = DAMPING / total
            at = n * X + x
            coef[0, at] = w * fxl
            coef[1, at] = w * fxh
            coef[2, at] = jnp.where(row == 0, 0.0, w * fyl)
            coef[3, at] = jnp.where(row == Y - 1, 0.0, w * fyh)
            coef[4, at] = jnp.where(col < step, 0.0, w * fzl)
            coef[5, at] = jnp.where(col >= Z - step, 0.0, w * fzh)
            coef[6, at] = w * gather_source[n, x]

    zero_plane = jnp.zeros((1, Y, Z), jnp.float32)

    def bottom(k, cur):
        new = KEEP * cur + coef[6]
        new += coef[0] * jnp.concatenate([zero_plane, cur[:-1]], axis=0)
        new += coef[1] * jnp.concatenate([cur[1:], zero_plane], axis=0)
        new += coef[2] * pltpu.roll(cur, 1, 1)
        new += coef[3] * pltpu.roll(cur, Y - 1, 1)
        new += coef[4] * pltpu.roll(cur, step, 2)
        new += coef[5] * pltpu.roll(cur, Z - step, 2)
        return new

    coef[7] = lax.fori_loop(0, BOTTOM - 1, bottom, coef[6], unroll=15)
    for x in range(X):
        answer[LEVELS][x] = coef[7, narrow * X + x]

    for level in reversed(range(LEVELS)):
        X, Y = dims(level)
        half = Y // 2

        def raised(x, level=level, Y=Y, half=half):
            e = answer[level + 1][x // 2]
            tmp[pl.ds(0, half, stride=2), :] = e
            tmp[pl.ds(1, half, stride=2), :] = e
            return iterates[level][1, x + 1, PAD : PAD + Y, :] + tmp[:Y, :]

        produce(level, 2, raised)
        produce(level, 3, lambda x, level=level: sweep(level, 2, x))
        target = out_ref if level == 0 else answer[level]

        def close(x, carry, level=level, target=target):
            target[x] = sweep(level, 3, x)
            return carry

        lax.fori_loop(0, X, close, 0, unroll=4)

    assert len(pushed) == len(shares)

    def end(k, carry):
        carry_landing(k).wait_recv()
        carry_copy(k).wait_send()
        return carry

    lax.fori_loop(1, owners, end, 0)
    lax.fori_loop(1, owners, solved_end, 0)
    own_copy.wait()
    face_drain()
    source_drain()
    for drain in drains:
        drain()


def f32(*shape):
    return pltpu.VMEM(shape, jnp.float32)


def call_solve(n_wide, n_narrow, receive_index, solved, carried):
    X3, Y3 = dims(LEVELS)
    levels = [dims(level) for level in range(LEVELS)]
    padded = f32(X0 + 2, Y0 + 2 * PAD, Z)
    each = [f32(X, Y, Z) for X, Y in levels]
    moves = 3 + 4 * LEVELS
    scratch = [
        f32(64, Z),
        f32(Y0, Z),
        padded,
        padded,
        f32(X0, Y0, Z),
        padded,
        f32(2, 2, X0, Z),
        f32(2, 2, X0, Z),
        [f32(4, X + 2, Y + 2 * PAD, Z) for X, Y in levels],
        [f32(4, 2, X, Z) for X, Y in levels],
        [f32(4, 2, X, Z) for X, Y in levels],
        [f32(X + 1, Y, Z) for X, Y in levels],
        each,
        each,
        each,
        each,
        each,
        each,
        each,
        [f32(*dims(level), Z) for level in range(LEVELS + 1)],
        f32(n_narrow, 5 * X3 + 1, Y3, Z),
        f32(n_narrow, X3, Y3, Z),
        f32(8, n_narrow * X3, Y3, Z),
        pltpu.SemaphoreType.DMA((moves, 4)),
        pltpu.SemaphoreType.DMA((moves, 4)),
        pltpu.SemaphoreType.DMA((2, n_narrow - 1)),
        pltpu.SemaphoreType.DMA((2, n_narrow - 1)),
        pltpu.SemaphoreType.DMA((n_wide * n_narrow,)),
        pltpu.SemaphoreType.DMA((n_wide * n_narrow,)),
        pltpu.SemaphoreType.DMA((2,)),
        pltpu.SemaphoreType.DMA((n_wide * n_narrow,)),
        pltpu.SemaphoreType.DMA((n_wide * n_narrow,)),
    ]
    return pl.pallas_call(
        functools.partial(solve_kernel, n_wide, n_narrow),
        out_shape=(
            jax.ShapeDtypeStruct((X0, Y0, Z), jnp.float32),
            jax.ShapeDtypeStruct(solved.shape, solved.dtype),
            jax.ShapeDtypeStruct(carried.shape, carried.dtype),
        ),
        in_specs=[
            pl.BlockSpec(memory_space=pltpu.SMEM),
            pl.BlockSpec(memory_space=pl.ANY),
            pl.BlockSpec(memory_space=pl.ANY),
        ],
        out_specs=(
            pl.BlockSpec(memory_space=pltpu.VMEM),
            pl.BlockSpec(memory_space=pltpu.VMEM),
            pl.BlockSpec(memory_space=pl.ANY),
        ),
        scratch_shapes=scratch,
        compiler_params=pltpu.CompilerParams(
            collective_id=0, has_side_effects=True, vmem_limit_bytes=VMEM_LIMIT
        ),
        cost_estimate=pl.CostEstimate(
            flops=200_000_000, bytes_accessed=200_000_000, transcendentals=0
        ),
    )(receive_index, solved, carried)


def shards(n_wide, n_narrow, target_slot, fields):
    per_owner, n_fields, cells = fields.shape
    owners = n_wide * n_narrow
    me = lax.axis_index("wide") * n_narrow + lax.axis_index("narrow")
    slots = owners * CAPACITY
    place = jnp.arange(per_owner, dtype=jnp.int32)
    own_target = lax.dynamic_slice_in_dim(target_slot, me * per_owner, per_owner) // per_owner
    earlier = jnp.sum(
        (
            (own_target[:, None] == own_target[None, :]) & (place[:, None] > place[None, :])
        ).astype(jnp.int32),
        axis=1,
    )
    own_slot = own_target * CAPACITY + earlier
    slot_ids = jnp.arange(slots, dtype=jnp.int32)
    send_index = jnp.sum(
        jnp.where(own_slot[None, :] == slot_ids[:, None], place[None, :], 0), axis=1
    )
    table = target_slot.reshape(owners, per_owner)
    to_me = table // per_owner == me
    rank = jnp.sum(
        (to_me[:, None, :] & (place[None, :, None] > place[None, None, :])).astype(jnp.int32),
        axis=2,
    )
    row = jnp.arange(owners, dtype=jnp.int32)[:, None] * CAPACITY + rank
    receive_index = jnp.sum(
        jnp.where(
            target_slot[None, :] == (me * per_owner + place)[:, None], row.reshape(-1)[None, :], 0
        ),
        axis=1,
    )

    smem = pl.BlockSpec(memory_space=pltpu.SMEM)
    vmem = pl.BlockSpec(memory_space=pltpu.VMEM)
    params = pltpu.CompilerParams(vmem_limit_bytes=VMEM_LIMIT)
    carried_fields = n_fields - SOLVED
    solved, carried = pl.pallas_call(
        pack_kernel,
        out_shape=(
            jax.ShapeDtypeStruct((slots, SOLVED, cells), fields.dtype),
            jax.ShapeDtypeStruct((slots, carried_fields, cells), fields.dtype),
        ),
        in_specs=[smem, vmem],
        out_specs=(vmem, vmem),
        compiler_params=params,
    )(send_index, fields)
    pressure, solved, carried = call_solve(n_wide, n_narrow, receive_index, solved, carried)
    migrated = pl.pallas_call(
        merge_kernel,
        out_shape=jax.ShapeDtypeStruct(fields.shape, fields.dtype),
        in_specs=[smem, vmem, vmem],
        out_specs=vmem,
        compiler_params=params,
    )(receive_index, solved, carried)
    return migrated, pressure


def solution(mesh):
    body = functools.partial(shards, mesh.shape["wide"], mesh.shape["narrow"])
    in_specs = (P(), P(("wide", "narrow"), None, None))
    out_specs = (P(("wide", "narrow"), None, None), P("narrow", "wide", None))
    return jax.shard_map(body, mesh=mesh, in_specs=in_specs, out_specs=out_specs, check_vma=False)
```

profile of v0, /device:TPU:0, one launch (start us, length us, event | category | flops | bytes accessed | tf_op | source)
XLA Modules:
  0.0 134.0 jit_solution(15719626455840530079)
XLA Ops:
  0.6 0.8 and_select_fusion
  1.4 0.2 convert_reduce_fusion.1
  1.6 0.8 multiply_add_fusion
  2.4 0.6 select_reduce_fusion.1.index_ref
  3.0 0.8 reshape.76
  3.8 0.6 convert_reduce_fusion
  4.4 0.1 broadcast_add_fusion
  4.5 0.1 add.45
  4.5 1.4 %select_reduce_fusion.index_ref = s32[32]{0:T(128)} fusion(s32[1024]{0:T(1024)S(1)} %add.45, s32[1024]{0:T(1024)} %param.2, s32[32]{0:T(128)S(1)} %iota_add_fusion), kind=kLoop, calls=%fused_computation.1 | loop fusion | flops 98272 | bytes 8448 | tf_op jit(solution)/shard_map/reduce_sum | solution.py:746
  5.9 4.1 %shard_map.41 = (bf16[64,4,4096]{2,1,0:T(4,128)(2,1)}, bf16[64,4,4096]{2,1,0:T(4,128)(2,1)}) custom-call(s32[64]{0:T(128)} %select_reduce_fusion.1.index_ref, bf16[32,8,4096]{2,1,0:T(8,128)(2,1)} %fields_ref.1), custom_call_target="tpu_custom_call" | custom-call | tf_op jit(solution)/shard_map/pallas_call | solution.py:757
  10.0 119.0 %shard_map.42 = (f32[16,64,128]{2,1,0:T(8,128)}, bf16[64,4,4096]{2,1,0:T(4,128)(2,1)}, bf16[64,4,4096]{2,1,0:T(4,128)(2,1)}) custom-call(s32[32]{0:T(128)} %select_reduce_fusion.index_ref, bf16[64,4,4096]{2,1,0:T(4,128)(2,1)} %get-tuple-element.7.solved_ref, bf16[64,4,4096]{2,1,0:T(4,128)(2,1)} %get-tuple-element.8.carried_ref), custom_call_target="tpu_custom_call" | custom-call | flops 200000000 | bytes 200000000 | tf_op jit(solution)/shard_map/pallas_call | solution.py:694
  129.1 0.0 copy-start
  129.1 4.2 %shard_map.43 = bf16[32,8,4096]{2,1,0:T(8,128)(2,1)} custom-call(s32[32]{0:T(128)} %select_reduce_fusion.index_ref, bf16[64,4,4096]{2,1,0:T(4,128)(2,1)} %get-tuple-element.9.solved_ref, bf16[64,4,4096]{2,1,0:T(4,128)(2,1)} %get-tuple-element.10.carried_ref), custom_call_target="tpu_custom_call" | custom-call | tf_op jit(solution)/shard_map/pallas_call | solution.py:768
  133.2 0.0 copy-done
  133.2 0.8 copy.5
  (3 shorter events, 0.0 us)
Async XLA Ops:
  129.1 4.2 %copy-start = (f32[16,64,128]{2,1,0:T(8,128)S(1)}, f32[16,64,128]{2,1,0:T(8,128)}, u32[]{:S(2)}) copy-start(f32[16,64,128]{2,1,0:T(8,128)} %get-tuple-element.17) | copy-start | bytes 1572868
where the time goes:
time: 134 us
  Pallas kernels  127 us (95%)
  other arithmetic  4.45 us (3%)
  local copies, waits for them, and re-layouts  1.63 us (1%)
    pallas_call x1, Pallas kernels, call_solve(): pl.pallas_call(functools.partial(solve_kernel, n_wide, n_narrow), out_sha...  119 us
    pallas_call x1, Pallas kernels, shards(): pl.pallas_call(merge_kernel, out_shape=jax.ShapeDtypeStruct(fields.shape,...  4.17 us
    pallas_call x1, Pallas kernels, shards(): pl.pallas_call(pack_kernel, out_shape=(jax.ShapeDtypeStruct((slots, SOLVE...  4.09 us

commit v1 on v0

v1 whole, which is shorter than its diff:
```python
import functools

import jax
import jax.numpy as jnp
from jax import lax
from jax.experimental import pallas as pl
from jax.experimental.pallas import tpu as pltpu
from jax.sharding import PartitionSpec as P

PATCH = 16
BYP = 4
BZP = 8
LEVELS = 3
BOTTOM = 16
DAMPING = 0.8
KEEP = 1.0 - DAMPING
SOLVED = 4
CAPACITY = 2
PER_OWNER = 32
X0 = PATCH
Y0 = PATCH * BYP
Z = PATCH * BZP
PAD = 8
EDGE = 4
HX = 2
HALO = (4, 2, 1)
FIELD_HALO = (3, 2, 2, 5)
HALO_PLANES = sum(FIELD_HALO)
CORNER = max(FIELD_HALO)
MESH = pl.DeviceIdType.MESH
VMEM_LIMIT = 60 * 1024 * 1024
SHARES = (2, 3, 4, 2, 2, 2, 2, 2, 2, 10)
OUT_GROUP = 8
SIDES = tuple((dx, dy) for dx in (-1, 0, 1) for dy in (-1, 0, 1) if dx or dy)


def dims(level):
    return X0 >> level, Y0 >> level


def solve_kernel(
    n_wide,
    n_narrow,
    target_ref,
    fields_ref,
    migrated_ref,
    pressure_ref,
    target,
    fields,
    solved,
    carried,
    arrived,
    moved,
    merged,
    pressure,
    send_index_v,
    receive_index_v,
    send_index,
    receive_index,
    turn,
    tmp,
    grids,
    sent_x,
    got_x,
    sent_y,
    got_y,
    sent_c,
    got_c,
    iterates,
    sent_rows,
    got_rows,
    face_x,
    face_y,
    face_zl,
    face_zh,
    inner_zl,
    inner_zh,
    diag,
    weight,
    source,
    answer,
    gather_faces,
    gather_source,
    coef,
    send_sem,
    recv_sem,
    gsend_sem,
    grecv_sem,
    carry_send_sem,
    carry_recv_sem,
    solved_send_sem,
    solved_recv_sem,
    local_sem,
    out_sem,
):
    wide = lax.axis_index("wide")
    narrow = lax.axis_index("narrow")
    owners = n_wide * n_narrow
    me = wide * n_narrow + narrow
    low = {-1: narrow > 0, 1: narrow < n_narrow - 1, 0: None}
    side_y = {-1: wide > 0, 1: wide < n_wide - 1, 0: None}

    def has(side):
        dx, dy = side
        if dx == 0:
            return side_y[dy]
        if dy == 0:
            return low[dx]
        return jnp.logical_and(low[dx], side_y[dy])

    def peer(side):
        return (wide + side[1], narrow + side[0])

    def back(side):
        return (-side[0], -side[1])

    others = [(wide, lax.rem(narrow + d, n_narrow)) for d in range(1, n_narrow)]

    target_copy = pltpu.make_async_copy(target_ref, target, local_sem.at[0])
    target_copy.start()
    fields_copy = pltpu.make_async_copy(fields_ref, fields, local_sem.at[1])
    fields_copy.start()

    def partner(k):
        distance = jnp.where(lax.rem(k, 2) == 1, owners // 2 + k // 2, k // 2)
        owner = jnp.bitwise_xor(me, distance)
        return owner, (owner // n_narrow, lax.rem(owner, n_narrow))

    barrier = pltpu.get_barrier_semaphore()

    def greet(k, carry):
        _, device = partner(k)
        pl.semaphore_signal(barrier, inc=1, device_id=device, device_id_type=MESH)
        return carry

    lax.fori_loop(1, owners, greet, 0)

    target_copy.wait()
    segments = Z // PER_OWNER
    own_row = target[pl.ds(me // segments, 1), :]
    lane_d = lax.broadcasted_iota(jnp.int32, (owners, Z), 1)
    owner_d = lax.broadcasted_iota(jnp.int32, (owners, Z), 0)
    mine = jnp.logical_and(
        lane_d // PER_OWNER == lax.rem(me, segments), own_row // PER_OWNER == owner_d
    )
    place = lax.rem(lane_d, PER_OWNER)
    low_place = jnp.min(jnp.where(mine, place, PER_OWNER - 1), axis=1, keepdims=True)
    high_place = jnp.max(jnp.where(mine, place, 0), axis=1, keepdims=True)
    send_index_v[0] = jnp.broadcast_to(low_place, (owners, Z))
    send_index_v[1] = jnp.broadcast_to(high_place, (owners, Z))
    index_copy = pltpu.make_async_copy(send_index_v, send_index, local_sem.at[2])
    index_copy.start()

    table = target[...]
    t_rows = table.shape[0]
    t_lane = lax.broadcasted_iota(jnp.int32, (t_rows, Z), 1)
    t_owner = lax.broadcasted_iota(jnp.int32, (t_rows, Z), 0) * segments + t_lane // PER_OWNER
    t_place = lax.rem(t_lane, PER_OWNER)
    seen = jnp.where(table // PER_OWNER == me, 1, 0)
    step = 1
    while step < PER_OWNER:
        seen = jnp.maximum(seen, jnp.where(t_place >= step, pltpu.roll(seen, step, 1), 0))
        step *= 2
    rank = jnp.where(t_place >= 1, pltpu.roll(seen, 1, 1), 0)
    slot = t_owner * CAPACITY + rank
    for q in range(PER_OWNER):
        hit = jnp.where(table == me * PER_OWNER + q, slot, 0)
        receive_index_v[q : q + 1, :] = jnp.max(hit, axis=0, keepdims=True)
    slots_q = jnp.max(receive_index_v[...], axis=1, keepdims=True)
    receive_index_v[...] = jnp.broadcast_to(slots_q, (PER_OWNER, Z))
    receive_copy = pltpu.make_async_copy(receive_index_v, receive_index, local_sem.at[3])
    receive_copy.start()

    index_copy.wait()
    fields_copy.wait()
    pl.semaphore_wait(barrier, owners - 1)

    def block(owner):
        return pl.ds(owner * CAPACITY, CAPACITY)

    def bulk(packed, landed, send, recv, k, incoming=False):
        owner, device = partner(k)
        return pltpu.make_async_remote_copy(
            src_ref=packed.at[block(me if incoming else owner)],
            dst_ref=landed.at[block(owner if incoming else me)],
            send_sem=send.at[k],
            recv_sem=recv.at[k],
            device_id=device,
            device_id_type=MESH,
        )

    solved_bulk = functools.partial(bulk, solved, arrived, solved_send_sem, solved_recv_sem)
    carried_bulk = functools.partial(bulk, carried, moved, carry_send_sem, carry_recv_sem)

    def pack_solved(k, carry):
        owner, _ = partner(k)
        for r in range(CAPACITY):
            solved[owner * CAPACITY + r] = fields[send_index[r, owner, 0], :SOLVED]
        solved_bulk(k).start()
        return carry

    def pack_carried(k, carry):
        owner, _ = partner(k)
        for r in range(CAPACITY):
            carried[owner * CAPACITY + r] = fields[send_index[r, owner, 0], SOLVED:]
        return carry

    lax.fori_loop(1, owners, pack_solved, 0)
    for r in range(CAPACITY):
        patch = fields[send_index[r, me, 0]]
        arrived[me * CAPACITY + r] = patch[:SOLVED]
        moved[me * CAPACITY + r] = patch[SOLVED:]
    lax.fori_loop(1, owners, pack_carried, 0)

    bounds = [
        1 + (owners - 1) * sum(SHARES[:k]) // sum(SHARES) for k in range(len(SHARES) + 1)
    ]
    pushed = []

    def push():
        turn_now = len(pushed)
        pushed.append(turn_now)
        if bounds[turn_now] == bounds[turn_now + 1]:
            return

        def begin(k, carry):
            carried_bulk(k).start()
            return carry

        lax.fori_loop(bounds[turn_now], bounds[turn_now + 1], begin, 0)

    for level in range(LEVELS):
        X, Y = dims(level)
        p = iterates[level]
        for e in (2,) if level == 0 else (0, 2):

            @pl.when(jnp.logical_not(low[-1]))
            def _(p=p, e=e, Y=Y):
                p[e, :HX] = jnp.zeros((HX, Y + 2 * PAD, Z), jnp.float32)

            @pl.when(jnp.logical_not(low[1]))
            def _(p=p, e=e, X=X, Y=Y):
                p[e, HX + X :] = jnp.zeros((HX, Y + 2 * PAD, Z), jnp.float32)

            @pl.when(jnp.logical_not(side_y[-1]))
            def _(p=p, e=e, X=X, Y=Y):
                p[e, :, :PAD] = jnp.zeros((X + 2 * HX, PAD, Z), jnp.float32)

            @pl.when(jnp.logical_not(side_y[1]))
            def _(p=p, e=e, X=X, Y=Y):
                p[e, :, PAD + Y :] = jnp.zeros((X + 2 * HX, PAD, Z), jnp.float32)

    receive_copy.wait()

    def solved_arrive(k, carry):
        solved_bulk(k, incoming=True).wait_recv()
        return carry

    lax.fori_loop(1, owners, solved_arrive, 0)
    push()

    lane = lax.broadcasted_iota(jnp.int32, (8, Z), 1)
    block_lane = lane // PATCH
    lower_bits = [(block_lane // s) % 2 == 1 for s in (1, 2, 4)]

    def to_grid(step, carry):
        b = step // X0
        i = step % X0
        at = pl.multiple_of(i * 2 * Z, 2 * Z)
        rows = []
        for c in range(BZP):
            both = arrived[receive_index[b * BZP + c, 0], :, pl.ds(at, 2 * Z)].astype(
                jnp.float32
            )
            rows.append(jnp.concatenate([both[:, :Z], both[:, Z:]], axis=0))
        for bit, s in zip(lower_bits, (1, 2, 4)):
            new = list(rows)
            for c in range(BZP):
                if c & s == 0:
                    lower, upper = rows[c], rows[c + s]
                    new[c] = jnp.where(bit, pltpu.roll(upper, PATCH * s, 1), lower)
                    new[c + s] = jnp.where(bit, upper, pltpu.roll(lower, Z - PATCH * s, 1))
            rows = new
        for j in range(8):
            turn[8 * j : 8 * j + 8, :] = rows[j]
        for half in range(2):
            y = pl.multiple_of(b * PATCH + half * 8, 8)
            for f, ref in enumerate(grids):
                values = turn[pl.ds(half * SOLVED + f, 8, stride=8), :]
                ref[i + FIELD_HALO[f], pl.ds(PAD + y, 8), :] = values
        return carry

    lax.fori_loop(0, BYP * X0, to_grid, 0, unroll=8)

    def known(side, values):
        return jnp.where(has(side), values.astype(jnp.float32), 0.0)

    planes = []
    for f, h in enumerate(FIELD_HALO):
        planes += [(f, h, j) for j in range(h)]
    for n, (f, h, j) in enumerate(planes):
        for side, x in ((0, j), (1, X0 - h + j)):
            sent_x[side, n] = grids[f][h + x, PAD : PAD + Y0, :].astype(jnp.bfloat16)
    at_row = lax.broadcasted_iota(jnp.int32, (PAD, Z), 0)

    def end_rows(end, x):
        y = (0, Y0 - PAD)[end]
        u, v, w, r = (
            grids[f][h + x, PAD + y : PAD + y + PAD, :] for f, h in enumerate(FIELD_HALO)
        )
        if end == 0:
            uvw = jnp.where(
                at_row < 2, u, jnp.where(at_row < 5, pltpu.roll(v, 2, 0), pltpu.roll(w, 5, 0))
            )
        else:
            uvw = jnp.where(
                at_row > 5, u, jnp.where(at_row > 2, pltpu.roll(v, 6, 0), pltpu.roll(w, 3, 0))
            )
        return r.astype(jnp.bfloat16), uvw.astype(jnp.bfloat16)

    def keep_rows(end, x, uvw, r):
        y = (0, PAD + Y0)[end]
        u, v, w = (
            (uvw, pltpu.roll(uvw, 2, 0), pltpu.roll(uvw, 5, 0)),
            (uvw, pltpu.roll(uvw, 6, 0), pltpu.roll(uvw, 3, 0)),
        )[end]
        for f, values in enumerate((u, v, w, r)):
            h = FIELD_HALO[f]
            if -h <= x < X0 + h:
                grids[f][h + x, y : y + PAD, :] = values

    for end in range(2):
        for i in range(X0):
            sent_y[end, i], sent_y[end, X0 + i] = end_rows(end, i)
        for j in range(CORNER):
            for side, x in ((0, j), (1, X0 - CORNER + j)):
                (
                    sent_c[2 * side + end, j],
                    sent_c[2 * side + end, CORNER + j],
                ) = end_rows(end, x)

    def field_refs(side):
        dx, dy = side
        if dy == 0:
            return sent_x.at[(dx + 1) // 2], got_x.at[(1 - dx) // 2]
        if dx == 0:
            return sent_y.at[(dy + 1) // 2], got_y.at[(1 - dy) // 2]
        return sent_c.at[dx + 1 + (dy + 1) // 2], got_c.at[1 - dx + (1 - dy) // 2]

    def level_refs(level, e):
        X, Y = dims(level)
        p = iterates[level]

        def refs(side):
            dx, dy = side
            if dx == 0:
                which = e // 2
                return (
                    sent_rows[level].at[which, (dy + 1) // 2],
                    got_rows[level].at[which, (1 - dy) // 2],
                )
            h = HX if dy == 0 else 1
            src_x, dst_x, n_x = {
                -1: (HX, HX + X, h),
                0: (HX, HX, X),
                1: (HX + X - h, HX - h, h),
            }[dx]
            src_y, dst_y, n_y = {
                -1: (PAD, PAD + Y, PAD),
                0: (PAD, PAD, Y),
                1: (Y, 0, PAD),
            }[dy]
            return (
                p.at[e, pl.ds(src_x, n_x), pl.ds(src_y, n_y)],
                p.at[e, pl.ds(dst_x, n_x), pl.ds(dst_y, n_y)],
            )

        return refs

    def pack_rows(level, e):
        X, Y = dims(level)
        p = iterates[level]
        for end, y, first_row in ((0, PAD, 0), (1, Y, 6)):
            for g in range(X // 4):
                tile = None
                for k in range(4):
                    rows = p[e, HX + 4 * g + k, y : y + PAD, :]
                    shift = (2 * k - first_row) % PAD
                    rows = pltpu.roll(rows, shift, 0) if shift else rows
                    tile = rows if tile is None else jnp.where(at_row >= 2 * k, rows, tile)
                sent_rows[level][e // 2, end, g] = tile

    def unpack_rows(level, e):
        X, Y = dims(level)
        p = iterates[level]
        for end, y, first_row in ((0, 0, 6), (1, PAD + Y, 0)):
            for g in range(X // 4):
                tile = known((0, 2 * end - 1), got_rows[level][e // 2, end, g])
                for k in range(4):
                    shift = (first_row - 2 * k) % PAD
                    p[e, HX + 4 * g + k, y : y + PAD, :] = (
                        pltpu.roll(tile, shift, 0) if shift else tile
                    )

    drains = []

    def level_exchange(level, e, move):
        pack_rows(level, e)
        exchange(level_refs(level, e), move)
        unpack_rows(level, e)

    def exchange(refs, move):
        def copy(side, incoming=False):
            src, dst = refs(back(side) if incoming else side)
            return pltpu.make_async_remote_copy(
                src_ref=src,
                dst_ref=dst,
                send_sem=send_sem.at[move, SIDES.index(side)],
                recv_sem=recv_sem.at[move, SIDES.index(side if incoming else back(side))],
                device_id=peer(side),
                device_id_type=MESH,
            )

        def each(act):
            for side in SIDES:

                @pl.when(has(side))
                def _(side=side):
                    act(side)

        each(lambda side: copy(side).start())
        push()
        each(lambda side: copy(side, incoming=True).wait_recv())
        drains.append(lambda: each(lambda side: copy(side).wait_send()))

    exchange(field_refs, 0)

    for n, (f, h, j) in enumerate(planes):
        for dx, x in ((-1, j), (1, h + X0 + j)):
            at = (dx + 1) // 2
            grids[f][x, PAD : PAD + Y0, :] = known((dx, 0), got_x[at, n])
    for end, dy in ((0, -1), (1, 1)):
        for i in range(X0):
            r, uvw = (known((0, dy), got_y[end, k * X0 + i]) for k in range(2))
            keep_rows(end, i, uvw, r)
        for j in range(CORNER):
            for side, dx, x in ((0, -1, j - CORNER), (1, 1, X0 + j)):
                r, uvw = (
                    known((dx, dy), got_c[2 * side + end, k * CORNER + j]) for k in range(2)
                )
                keep_rows(end, x, uvw, r)

    def lanes(values):
        return lax.broadcasted_iota(jnp.int32, values.shape, 1)

    def z_low(values, step):
        return jnp.where(lanes(values) < step, 0.0, pltpu.roll(values, step, 1))

    def z_high(values, step):
        return jnp.where(lanes(values) >= Z - step, 0.0, pltpu.roll(values, Z - step, 1))

    def keep_inner(level, i, zl, zh):
        step = 1 << level
        inner_zl[level][i] = jnp.where(lanes(zl) < step, 0.0, zl)
        inner_zh[level][i] = jnp.where(lanes(zh) >= Z - step, 0.0, zh)

    push()
    grid_u, grid_v, grid_w, grid_r = grids
    rows0 = Y0 + 2 * EDGE
    win0 = pl.ds(PAD - EDGE, rows0)

    def face(a, b):
        return 2.0 / jnp.maximum(a + b, 0.5)

    def faces(i, carry):
        here = grid_r[i + 1, win0, :]
        face_x[0][i] = face(grid_r[i, win0, :], here)
        face_y[0][i, :rows0, :] = face(grid_r[i + 1, pl.ds(PAD - EDGE - 1, rows0), :], here)
        last = PAD + EDGE + Y0
        face_y[0][i, rows0 : rows0 + EDGE, :] = face(
            grid_r[i + 1, last - 1 : last + EDGE - 1, :], grid_r[i + 1, last : last + EDGE, :]
        )
        zl, zh = face(z_low(here, 1), here), face(z_high(here, 1), here)
        face_zl[0][i] = zl
        face_zh[0][i] = zh
        keep_inner(0, i, zl, zh)
        return carry

    n_faces = X0 + 2 * HALO[0]
    lax.fori_loop(0, n_faces, faces, 0, unroll=4)
    face_x[0][n_faces] = face(grid_r[n_faces, win0, :], grid_r[n_faces + 1, win0, :])

    def inside_rows(level):
        Y = dims(level)[1]
        at = lax.broadcasted_iota(jnp.int32, (Y + 2 * EDGE, Z), 0)
        return jnp.logical_and(
            jnp.logical_or(side_y[-1], at >= EDGE), jnp.logical_or(side_y[1], at < EDGE + Y)
        )

    def weigh(level, i):
        X, Y = dims(level)
        h, rows = HALO[level], Y + 2 * EDGE
        total = face_x[level][i] + face_x[level][i + 1]
        total += face_y[level][i, :rows, :] + face_y[level][i, pl.ds(1, rows), :]
        total += face_zl[level][i] + face_zh[level][i]
        inside = jnp.logical_and(
            jnp.logical_or(low[-1], i >= h), jnp.logical_or(low[1], i < h + X)
        )
        w = jnp.where(jnp.logical_and(inside_rows(level), inside), DAMPING / total, 0.0)
        diag[level][i] = total
        weight[level][i] = w
        return w

    def first(j, carry):
        w = weigh(0, j + HALO[0] - HX)
        wz = grid_w[j + FIELD_HALO[2] - HX, win0, :]
        u_at, v_at = j + FIELD_HALO[0] - HX, j + FIELD_HALO[1] - HX
        du = grid_u[u_at + 1, win0, :] - grid_u[u_at - 1, win0, :]
        dv = (
            grid_v[v_at, pl.ds(PAD - EDGE + 1, rows0), :]
            - grid_v[v_at, pl.ds(PAD - EDGE - 1, rows0), :]
        )
        b = -0.5 * ((du + dv) + (z_high(wz, 1) - z_low(wz, 1)))
        source[0][j] = b
        iterates[0][0, j, win0, :] = w * b
        return carry

    lax.fori_loop(0, X0 + 2 * HX, first, 0, unroll=4)

    def z_bit(values, level):
        return (lanes(values) // (1 << level)) % 2 == 1

    def z_pair(values, level):
        step = 1 << level
        return values + jnp.where(
            z_bit(values, level), pltpu.roll(values, step, 1), pltpu.roll(values, Z - step, 1)
        )

    def z_even(values, level):
        return jnp.where(z_bit(values, level), pltpu.roll(values, 1 << level, 1), values)

    def z_odd(values, level):
        return jnp.where(z_bit(values, level), values, pltpu.roll(values, Z - (1 << level), 1))

    def coarse_faces(level, base, start, count, more=0):
        even = pl.ds(start, count, stride=2)
        even_y = pl.ds(start, count + more, stride=2)
        odd = pl.ds(start + 1, count, stride=2)
        after = pl.ds(start + 2, count, stride=2)
        fx, fy, zl, zh = (f[level] for f in (face_x, face_y, face_zl, face_zh))

        def cx(x):
            i = base + 2 * x
            return 0.25 * z_pair(fx[i, even, :] + fx[i, odd, :], level)

        def cy(x, rows):
            i = base + 2 * x
            return 0.25 * z_pair(fy[i, rows, :] + fy[i + 1, rows, :], level)

        def four(f, x):
            i = base + 2 * x
            return 0.25 * (
                (f[i, even, :] + f[i, odd, :]) + (f[i + 1, even, :] + f[i + 1, odd, :])
            )

        return (
            cx,
            lambda x: cy(x, even_y),
            lambda x: cy(x, after),
            lambda x: z_even(four(zl, x), level),
            lambda x: z_odd(four(zh, x), level),
        )

    for level in range(LEVELS - 1):
        X, Y = dims(level + 1)
        count = Y + EDGE
        n_planes = X + 2 * HALO[level + 1]
        cx, cyl, _, czl, czh = coarse_faces(level, 0, 0, count, more=1)
        rows = pl.ds(EDGE // 2, count)

        def coarsen(i, carry, level=level, rows=rows, count=count, cx=cx, cyl=cyl, czl=czl, czh=czh):
            face_x[level + 1][i, rows, :] = cx(i)
            face_y[level + 1][i, pl.ds(EDGE // 2, count + 1), :] = cyl(i)
            zl, zh = czl(i), czh(i)
            face_zl[level + 1][i, rows, :] = zl
            face_zh[level + 1][i, rows, :] = zh
            step = 1 << (level + 1)
            inner_zl[level + 1][i, rows, :] = jnp.where(lanes(zl) < step, 0.0, zl)
            inner_zh[level + 1][i, rows, :] = jnp.where(lanes(zh) >= Z - step, 0.0, zh)
            return carry

        lax.fori_loop(0, n_planes, coarsen, 0, unroll=3)
        face_x[level + 1][n_planes, rows, :] = cx(n_planes)

        def weigh_plane(i, carry, level=level):
            weigh(level + 1, i)
            return carry

        lax.fori_loop(0, n_planes, weigh_plane, 0, unroll=3)

    X, Y = dims(LEVELS)
    cx, cyl, cyh, czl, czh = coarse_faces(LEVELS - 1, HALO[LEVELS - 1], EDGE, Y)
    for x in range(X + 1):
        gather_faces[narrow, x] = cx(x)
    for x in range(X):
        for k, part in enumerate((cyl, cyh, czl, czh)):
            gather_faces[narrow, X + 1 + k * X + x] = part(x)

    def gather(ref, which):
        def copy(d, incoming=False):
            came = lax.rem(narrow + n_narrow - d, n_narrow) if incoming else narrow
            return pltpu.make_async_remote_copy(
                src_ref=ref.at[narrow],
                dst_ref=ref.at[came],
                send_sem=gsend_sem.at[which, d - 1],
                recv_sem=grecv_sem.at[which, d - 1],
                device_id=others[d - 1],
                device_id_type=MESH,
            )

        def start():
            for d in range(1, n_narrow):
                copy(d).start()

        def finish():
            for d in range(1, n_narrow):
                copy(d, incoming=True).wait_recv()

        def drain():
            for d in range(1, n_narrow):
                copy(d).wait_send()

        return start, finish, drain

    face_start, face_finish, face_drain = gather(gather_faces, 0)
    source_start, source_finish, source_drain = gather(gather_source, 1)
    face_start()

    def neighbour_sum(level, e, x, own):
        Y = dims(level)[1]
        p = iterates[level]
        step = 1 << level
        edge = 0 if own else EDGE
        start, rows = PAD - edge, Y + 2 * edge
        at = pl.ds(EDGE - edge, rows)
        i, j = x + HALO[level], x + HX
        here = p[e, j, pl.ds(start, rows), :]
        total = (
            face_x[level][i, at, :] * p[e, j - 1, pl.ds(start, rows), :]
            + face_x[level][i + 1, at, :] * p[e, j + 1, pl.ds(start, rows), :]
        )
        total += face_y[level][i, at, :] * p[e, j, pl.ds(start - 1, rows), :]
        total += face_y[level][i, pl.ds(EDGE - edge + 1, rows), :] * p[
            e, j, pl.ds(start + 1, rows), :
        ]
        total += inner_zl[level][i, at, :] * pltpu.roll(here, step, 1)
        total += inner_zh[level][i, at, :] * pltpu.roll(here, Z - step, 1)
        return here, total

    def sweep(level, e, x, own):
        Y = dims(level)[1]
        edge = 0 if own else EDGE
        here, total = neighbour_sum(level, e, x, own)
        w = weight[level][x + HALO[level], pl.ds(EDGE - edge, Y + 2 * edge), :]
        if e == 0:
            return (1.0 + KEEP) * here + w * total
        start = iterates[level][0, x + HX, pl.ds(PAD - edge, Y + 2 * edge), :]
        return (KEEP * here + start) + w * total

    def wide_sweep(level, e):
        X, Y = dims(level)

        def plane(j, carry):
            iterates[level][e + 1, j + HX - 1, pl.ds(PAD - EDGE, Y + 2 * EDGE), :] = sweep(
                level, e, j - 1, False
            )
            return carry

        lax.fori_loop(0, X + 2, plane, 0, unroll=3 if level == 0 else 2)

    for level in range(LEVELS):
        X, Y = dims(level)
        if level > 0:
            level_exchange(level, 0, level)
        wide_sweep(level, 0)
        h, half, last = HALO[level], Y // 2, level + 1 == LEVELS
        own_rows = pl.ds(EDGE, Y)

        def restrict(x, carry, level=level, Y=Y, h=h, half=half, last=last, own_rows=own_rows):
            both = None
            for k in range(2):
                fine = 2 * x + k
                here, total = neighbour_sum(level, 1, fine, True)
                b = source[0][fine + HX, own_rows, :] if level == 0 else source[level][fine]
                left = (b - diag[level][fine + h, own_rows, :] * here) + total
                both = left if both is None else both + left
            tmp[:Y, :] = both
            summed = (
                tmp[pl.ds(0, half, stride=2), :] + tmp[pl.ds(1, half, stride=2), :]
            )
            summed = 0.5 * z_pair(summed, level)
            if last:
                gather_source[narrow, x] = summed
            else:
                source[level + 1][x] = summed
                w = weight[level + 1][x + HALO[level + 1], pl.ds(EDGE, half), :]
                iterates[level + 1][0, x + HX, pl.ds(PAD, half), :] = w * summed
            return carry

        if last:
            for x in range(X // 2):
                restrict(x, 0)
        else:
            lax.fori_loop(0, X // 2, restrict, 0, unroll=4)

    source_start()
    push()
    face_finish()
    source_finish()
    X, Y = dims(LEVELS)
    step = 1 << LEVELS
    row = lax.broadcasted_iota(jnp.int32, (Y, Z), 0)
    col = lax.broadcasted_iota(jnp.int32, (Y, Z), 1)
    for n in range(n_narrow):
        for x in range(X):
            fxl, fxh = gather_faces[n, x], gather_faces[n, x + 1]
            fyl, fyh, fzl, fzh = (gather_faces[n, X + 1 + k * X + x] for k in range(4))
            total = ((fxl + fxh) + (fyl + fyh)) + (fzl + fzh)
            w = DAMPING / total
            at = n * X + x
            coef[0, at] = w * fxl
            coef[1, at] = w * fxh
            coef[2, at] = jnp.where(row == 0, 0.0, w * fyl)
            coef[3, at] = jnp.where(row == Y - 1, 0.0, w * fyh)
            coef[4, at] = jnp.where(col < step, 0.0, w * fzl)
            coef[5, at] = jnp.where(col >= Z - step, 0.0, w * fzh)
            coef[6, at] = w * gather_source[n, x]

    zero_plane = jnp.zeros((1, Y, Z), jnp.float32)

    def bottom(k, cur):
        new = KEEP * cur + coef[6]
        new += coef[0] * jnp.concatenate([zero_plane, cur[:-1]], axis=0)
        new += coef[1] * jnp.concatenate([cur[1:], zero_plane], axis=0)
        new += coef[2] * pltpu.roll(cur, 1, 1)
        new += coef[3] * pltpu.roll(cur, Y - 1, 1)
        new += coef[4] * pltpu.roll(cur, step, 2)
        new += coef[5] * pltpu.roll(cur, Z - step, 2)
        return new

    push()
    coef[7] = lax.fori_loop(0, BOTTOM - 1, bottom, coef[6], unroll=15)
    for x in range(X):
        answer[LEVELS][x] = coef[7, narrow * X + x]

    for level in reversed(range(LEVELS)):
        X, Y = dims(level)
        half = Y // 2

        def raised(x, carry, level=level, Y=Y, half=half):
            e = answer[level + 1][x // 2]
            tmp[pl.ds(0, half, stride=2), :] = e
            tmp[pl.ds(1, half, stride=2), :] = e
            iterates[level][2, x + HX, PAD : PAD + Y, :] = (
                iterates[level][1, x + HX, PAD : PAD + Y, :] + tmp[:Y, :]
            )
            return carry

        lax.fori_loop(0, X, raised, 0, unroll=4)
        level_exchange(level, 2, LEVELS + level)
        wide_sweep(level, 2)
        result = pressure if level == 0 else answer[level]

        def close(x, carry, level=level, result=result):
            result[x] = sweep(level, 3, x, True)
            return carry

        lax.fori_loop(0, X, close, 0, unroll=4)

    assert len(pushed) == len(SHARES)
    pressure_copy = pltpu.make_async_copy(pressure, pressure_ref, local_sem.at[4])
    pressure_copy.start()

    def merge_solved(q, carry):
        merged[q, :SOLVED] = arrived[receive_index[q, 0]]
        return carry

    lax.fori_loop(0, PER_OWNER, merge_solved, 0, unroll=4)

    def carried_arrive(k, carry):
        carried_bulk(k, incoming=True).wait_recv()
        return carry

    lax.fori_loop(1, owners, carried_arrive, 0)

    def out_copy(g):
        group = pl.ds(g * OUT_GROUP, OUT_GROUP)
        return pltpu.make_async_copy(merged.at[group], migrated_ref.at[group], out_sem.at[g])

    for g in range(PER_OWNER // OUT_GROUP):

        def merge_carried(q, carry):
            merged[q, SOLVED:] = moved[receive_index[q, 0]]
            return carry

        lax.fori_loop(g * OUT_GROUP, (g + 1) * OUT_GROUP, merge_carried, 0, unroll=4)
        out_copy(g).start()

    def end(k, carry):
        carried_bulk(k).wait_send()
        solved_bulk(k).wait_send()
        return carry

    lax.fori_loop(1, owners, end, 0)
    face_drain()
    source_drain()
    for drain in drains:
        drain()
    pressure_copy.wait()
    for g in range(PER_OWNER // OUT_GROUP):
        out_copy(g).wait()


def f32(*shape):
    return pltpu.VMEM(shape, jnp.float32)


def bf16(*shape):
    return pltpu.VMEM(shape, jnp.bfloat16)


def call_solve(n_wide, n_narrow, table, fields):
    per_owner, n_fields, cells = fields.shape
    owners = n_wide * n_narrow
    slots = owners * CAPACITY
    X3, Y3 = dims(LEVELS)
    levels = [(level, *dims(level)) for level in range(LEVELS)]
    faces = [f32(X + 2 * HALO[l], Y + 2 * EDGE, Z) for l, X, Y in levels]
    moves = 2 * LEVELS
    packs = {
        "solved": bf16(slots, SOLVED, cells),
        "carried": bf16(slots, n_fields - SOLVED, cells),
    }
    dma = pltpu.SemaphoreType.DMA
    scratch = [
        pltpu.VMEM(table.shape, jnp.int32),
        bf16(*fields.shape),
        packs["solved"],
        packs["carried"],
        packs["solved"],
        packs["carried"],
        bf16(*fields.shape),
        f32(X0, Y0, Z),
        pltpu.VMEM((CAPACITY, owners, Z), jnp.int32),
        pltpu.VMEM((per_owner, Z), jnp.int32),
        pltpu.SMEM((CAPACITY, owners, Z), jnp.int32),
        pltpu.SMEM((per_owner, Z), jnp.int32),
        f32(64, Z),
        f32(Y0, Z),
        [f32(X0 + 2 * h, Y0 + 2 * PAD, Z) for h in FIELD_HALO],
        bf16(2, HALO_PLANES, Y0, Z),
        bf16(2, HALO_PLANES, Y0, Z),
        bf16(2, 2 * X0, PAD, Z),
        bf16(2, 2 * X0, PAD, Z),
        bf16(4, 2 * CORNER, PAD, Z),
        bf16(4, 2 * CORNER, PAD, Z),
        [f32(4, X + 2 * HX, Y + 2 * PAD, Z) for l, X, Y in levels],
        [f32(2, 2, X // 4, PAD, Z) for l, X, Y in levels],
        [f32(2, 2, X // 4, PAD, Z) for l, X, Y in levels],
        [f32(X + 2 * HALO[l] + 1, Y + 2 * EDGE, Z) for l, X, Y in levels],
        [f32(X + 2 * HALO[l], Y + 2 * EDGE + 8, Z) for l, X, Y in levels],
        faces,
        faces,
        faces,
        faces,
        faces,
        faces,
        [f32(X0 + 2 * HX, Y0 + 2 * EDGE, Z)] + [f32(X, Y, Z) for l, X, Y in levels[1:]],
        [f32(*dims(level), Z) for level in range(LEVELS + 1)],
        f32(n_narrow, 5 * X3 + 1, Y3, Z),
        f32(n_narrow, X3, Y3, Z),
        f32(8, n_narrow * X3, Y3, Z),
        dma((moves, 8)),
        dma((moves, 8)),
        dma((2, n_narrow - 1)),
        dma((2, n_narrow - 1)),
        dma((owners,)),
        dma((owners,)),
        dma((owners,)),
        dma((owners,)),
        dma((5,)),
        dma((per_owner // OUT_GROUP,)),
    ]
    anywhere = pl.BlockSpec(memory_space=pl.ANY)
    return pl.pallas_call(
        functools.partial(solve_kernel, n_wide, n_narrow),
        out_shape=(
            jax.ShapeDtypeStruct(fields.shape, fields.dtype),
            jax.ShapeDtypeStruct((X0, Y0, Z), jnp.float32),
        ),
        in_specs=[anywhere, anywhere],
        out_specs=(anywhere, anywhere),
        scratch_shapes=scratch,
        compiler_params=pltpu.CompilerParams(
            collective_id=0, has_side_effects=True, vmem_limit_bytes=VMEM_LIMIT
        ),
        cost_estimate=pl.CostEstimate(
            flops=200_000_000, bytes_accessed=200_000_000, transcendentals=0
        ),
    )(table, fields)


def shards(n_wide, n_narrow, target_slot, fields):
    return call_solve(n_wide, n_narrow, target_slot.reshape(-1, Z), fields)


def solution(mesh):
    body = functools.partial(shards, mesh.shape["wide"], mesh.shape["narrow"])
    in_specs = (P(), P(("wide", "narrow"), None, None))
    out_specs = (P(("wide", "narrow"), None, None), P("narrow", "wide", None))
    return jax.shard_map(body, mesh=mesh, in_specs=in_specs, out_specs=out_specs, check_vma=False)
```

time: 134 us -> 126 us (0.940); the launches traced: 134 us -> 124 us
  Pallas kernels: 127 us -> 119 us
  other arithmetic: 4.45 us -> 0 us
  local copies, waits for them, and re-layouts: 1.63 us -> 3.98 us
    pallas_call x2 -> x0, Pallas kernels: 8.26 us -> none  [the longest x1 4.17 us: shards(): pl.pallas_call(merge_kernel, out_shape=jax.ShapeDtypeStruct(fields.shape,...]
    unnamed x3 -> x4, local copies, waits for them, and re-layouts: 0.8 us -> 3.98 us
    reduce_sum x4 -> x0, other arithmetic: 2.8 us -> none  [the longest x1 1.39 us: shards(): jnp.sum(jnp.where(target_slot[None, :] == (me * per_owner + place)[:, Non...]
where the time goes in v1:
time: 126 us; the launch traced here: 124 us
  Pallas kernels  119 us (94%)
  local copies, waits for them, and re-layouts  3.98 us (3%)
    pallas_call x1, Pallas kernels, call_solve(): pl.pallas_call(functools.partial(solve_kernel, n_wide, n_narrow), out_sha...  119 us
    unnamed x4, local copies, waits for them, and re-layouts  3.98 us

profile of v1, /device:TPU:0, one launch (start us, length us, event | category | flops | bytes accessed | tf_op | source)
XLA Modules:
  0.0 124.0 jit_solution(11807640225842577762)
XLA Ops:
  0.6 119.4 %shard_map.41 = (bf16[32,8,4096]{2,1,0:T(8,128)(2,1)}, f32[16,64,128]{2,1,0:T(8,128)}) custom-call(s32[8,128]{1,0:T(8,128)} %bitcast.1, bf16[32,8,4096]{2,1,0:T(8,128)(2,1)} %fields_ref.1), custom_call_target="tpu_custom_call" | custom-call | flops 200000000 | bytes 200000000 | tf_op jit(solution)/shard_map/pallas_call | solution.py:895
  120.0 0.0 copy-start
  120.0 3.2 %copy.6 = bf16[32,8,4096]{2,1,0:T(8,128)(2,1)} copy(bf16[32,8,4096]{2,1,0:T(8,128)(2,1)} %get-tuple-element.4) | data formatting | bytes 4194304
  123.2 0.0 copy-done
  123.2 0.8 copy.7
Async XLA Ops:
  120.0 3.2 %copy-start = (f32[16,64,128]{2,1,0:T(8,128)S(1)}, f32[16,64,128]{2,1,0:T(8,128)}, u32[]{:S(2)}) copy-start(f32[16,64,128]{2,1,0:T(8,128)} %get-tuple-element.5) | copy-start | bytes 1572868

commit v2 on v1

--- a/solution.py
+++ b/solution.py
@@ -22,15 +22,17 @@
 Z = PATCH * BZP
 PAD = 8
 EDGE = 4
-HX = 2
+HX = (2, 3, 2)
+ROWS = (2, 4, 2)
+CORNER_PLANES = (1, 3, 1)
 HALO = (4, 2, 1)
 FIELD_HALO = (3, 2, 2, 5)
 HALO_PLANES = sum(FIELD_HALO)
 CORNER = max(FIELD_HALO)
 MESH = pl.DeviceIdType.MESH
-VMEM_LIMIT = 60 * 1024 * 1024
-SHARES = (2, 3, 4, 2, 2, 2, 2, 2, 2, 10)
+SHARES = (1, 1, 2, 1, 1, 1, 1, 1, 7)
 OUT_GROUP = 8
+PIECES = 8
 SIDES = tuple((dx, dy) for dx in (-1, 0, 1) for dy in (-1, 0, 1) if dx or dy)
 
 
@@ -79,6 +81,7 @@
     weight,
     source,
     answer,
+    near_answer,
     gather_faces,
     gather_source,
     coef,
@@ -121,10 +124,12 @@
     fields_copy = pltpu.make_async_copy(fields_ref, fields, local_sem.at[1])
     fields_copy.start()
 
-    def partner(k):
-        distance = jnp.where(lax.rem(k, 2) == 1, owners // 2 + k // 2, k // 2)
+    def at_distance(distance):
         owner = jnp.bitwise_xor(me, distance)
         return owner, (owner // n_narrow, lax.rem(owner, n_narrow))
+
+    def partner(k):
+        return at_distance(jnp.where(lax.rem(k, 2) == 1, owners // 2 + k // 2, k // 2))
 
     barrier = pltpu.get_barrier_semaphore()
 
@@ -178,8 +183,8 @@
     def block(owner):
         return pl.ds(owner * CAPACITY, CAPACITY)
 
-    def bulk(packed, landed, send, recv, k, incoming=False):
-        owner, device = partner(k)
+    def bulk(whom, packed, landed, send, recv, k, incoming=False):
+        owner, device = whom(k)
         return pltpu.make_async_remote_copy(
             src_ref=packed.at[block(me if incoming else owner)],
             dst_ref=landed.at[block(owner if incoming else me)],
@@ -189,8 +194,8 @@
             device_id_type=MESH,
         )
 
-    solved_bulk = functools.partial(bulk, solved, arrived, solved_send_sem, solved_recv_sem)
-    carried_bulk = functools.partial(bulk, carried, moved, carry_send_sem, carry_recv_sem)
+    solved_bulk = functools.partial(bulk, partner, solved, arrived, solved_send_sem, solved_recv_sem)
+    carried_bulk = functools.partial(bulk, at_distance, carried, moved, carry_send_sem, carry_recv_sem)
 
     def pack_solved(k, carry):
         owner, _ = partner(k)
@@ -200,7 +205,7 @@
         return carry
 
     def pack_carried(k, carry):
-        owner, _ = partner(k)
+        owner, _ = at_distance(k)
         for r in range(CAPACITY):
             carried[owner * CAPACITY + r] = fields[send_index[r, owner, 0], SOLVED:]
         return carry
@@ -212,8 +217,9 @@
         moved[me * CAPACITY + r] = patch[SOLVED:]
     lax.fori_loop(1, owners, pack_carried, 0)
 
-    bounds = [
-        1 + (owners - 1) * sum(SHARES[:k]) // sum(SHARES) for k in range(len(SHARES) + 1)
+    half_way = owners // 2
+    bounds = [1] + [
+        half_way + half_way * sum(SHARES[:k]) // sum(SHARES) for k in range(len(SHARES) + 1)
     ]
     pushed = []
 
@@ -229,26 +235,28 @@
 
         lax.fori_loop(bounds[turn_now], bounds[turn_now + 1], begin, 0)
 
+    push()
     for level in range(LEVELS):
         X, Y = dims(level)
         p = iterates[level]
+        hx = HX[level]
         for e in (2,) if level == 0 else (0, 2):
 
             @pl.when(jnp.logical_not(low[-1]))
-            def _(p=p, e=e, Y=Y):
-                p[e, :HX] = jnp.zeros((HX, Y + 2 * PAD, Z), jnp.float32)
+            def _(p=p, e=e, Y=Y, hx=hx):
+                p[e, :hx] = jnp.zeros((hx, Y + 2 * PAD, Z), jnp.float32)
 
             @pl.when(jnp.logical_not(low[1]))
-            def _(p=p, e=e, X=X, Y=Y):
-                p[e, HX + X :] = jnp.zeros((HX, Y + 2 * PAD, Z), jnp.float32)
+            def _(p=p, e=e, X=X, Y=Y, hx=hx):
+                p[e, hx + X :] = jnp.zeros((hx, Y + 2 * PAD, Z), jnp.float32)
 
             @pl.when(jnp.logical_not(side_y[-1]))
-            def _(p=p, e=e, X=X, Y=Y):
-                p[e, :, :PAD] = jnp.zeros((X + 2 * HX, PAD, Z), jnp.float32)
+            def _(p=p, e=e, X=X, Y=Y, hx=hx):
+                p[e, :, :PAD] = jnp.zeros((X + 2 * hx, PAD, Z), jnp.float32)
 
             @pl.when(jnp.logical_not(side_y[1]))
-            def _(p=p, e=e, X=X, Y=Y):
-                p[e, :, PAD + Y :] = jnp.zeros((X + 2 * HX, PAD, Z), jnp.float32)
+            def _(p=p, e=e, X=X, Y=Y, hx=hx):
+                p[e, :, PAD + Y :] = jnp.zeros((X + 2 * hx, PAD, Z), jnp.float32)
 
     receive_copy.wait()
 
@@ -347,23 +355,24 @@
             return sent_y.at[(dy + 1) // 2], got_y.at[(1 - dy) // 2]
         return sent_c.at[dx + 1 + (dy + 1) // 2], got_c.at[1 - dx + (1 - dy) // 2]
 
-    def level_refs(level, e):
+    def level_refs(level, e, into):
         X, Y = dims(level)
         p = iterates[level]
+        hx = HX[level]
 
         def refs(side):
             dx, dy = side
             if dx == 0:
-                which = e // 2
+                which = into // 2
                 return (
                     sent_rows[level].at[which, (dy + 1) // 2],
                     got_rows[level].at[which, (1 - dy) // 2],
                 )
-            h = HX if dy == 0 else 1
+            h = hx if dy == 0 else CORNER_PLANES[level]
             src_x, dst_x, n_x = {
-                -1: (HX, HX + X, h),
-                0: (HX, HX, X),
-                1: (HX + X - h, HX - h, h),
+                -1: (hx, hx + X, h),
+                0: (hx, hx, X),
+                1: (hx + X - h, hx - h, h),
             }[dx]
             src_y, dst_y, n_y = {
                 -1: (PAD, PAD + Y, PAD),
@@ -372,42 +381,39 @@
             }[dy]
             return (
                 p.at[e, pl.ds(src_x, n_x), pl.ds(src_y, n_y)],
-                p.at[e, pl.ds(dst_x, n_x), pl.ds(dst_y, n_y)],
+                p.at[into, pl.ds(dst_x, n_x), pl.ds(dst_y, n_y)],
             )
 
         return refs
 
-    def pack_rows(level, e):
+    def pack_rows(level, e, into):
         X, Y = dims(level)
-        p = iterates[level]
-        for end, y, first_row in ((0, PAD, 0), (1, Y, 6)):
-            for g in range(X // 4):
+        p, n = iterates[level], ROWS[level]
+        per = PAD // n
+        for end, y, first_row in ((0, PAD, 0), (1, Y, PAD - n)):
+            for g in range(X // per):
                 tile = None
-                for k in range(4):
-                    rows = p[e, HX + 4 * g + k, y : y + PAD, :]
-                    shift = (2 * k - first_row) % PAD
+                for k in range(per):
+                    rows = p[e, HX[level] + per * g + k, y : y + PAD, :]
+                    shift = (n * k - first_row) % PAD
                     rows = pltpu.roll(rows, shift, 0) if shift else rows
-                    tile = rows if tile is None else jnp.where(at_row >= 2 * k, rows, tile)
-                sent_rows[level][e // 2, end, g] = tile
-
-    def unpack_rows(level, e):
+                    tile = rows if tile is None else jnp.where(at_row >= n * k, rows, tile)
+                sent_rows[level][into // 2, end, g] = tile
+
+    def unpack_rows(level, into):
         X, Y = dims(level)
-        p = iterates[level]
-        for end, y, first_row in ((0, 0, 6), (1, PAD + Y, 0)):
-            for g in range(X // 4):
-                tile = known((0, 2 * end - 1), got_rows[level][e // 2, end, g])
-                for k in range(4):
-                    shift = (first_row - 2 * k) % PAD
-                    p[e, HX + 4 * g + k, y : y + PAD, :] = (
+        p, n = iterates[level], ROWS[level]
+        per = PAD // n
+        for end, y, first_row in ((0, 0, PAD - n), (1, PAD + Y, 0)):
+            for g in range(X // per):
+                tile = known((0, 2 * end - 1), got_rows[level][into // 2, end, g])
+                for k in range(per):
+                    shift = (first_row - n * k) % PAD
+                    p[into, HX[level] + per * g + k, y : y + PAD, :] = (
                         pltpu.roll(tile, shift, 0) if shift else tile
                     )
 
     drains = []
-
-    def level_exchange(level, e, move):
-        pack_rows(level, e)
-        exchange(level_refs(level, e), move)
-        unpack_rows(level, e)
 
     def exchange(refs, move):
         def copy(side, incoming=False):
@@ -428,12 +434,113 @@
                 def _(side=side):
                     act(side)
 
-        each(lambda side: copy(side).start())
-        push()
-        each(lambda side: copy(side, incoming=True).wait_recv())
         drains.append(lambda: each(lambda side: copy(side).wait_send()))
-
-    exchange(field_refs, 0)
+        return (
+            lambda: each(lambda side: copy(side).start()),
+            lambda: each(lambda side: copy(side, incoming=True).wait_recv()),
+        )
+
+    def level_exchange(level, e, into, move):
+        pack_rows(level, e, into)
+        start, arrive = exchange(level_refs(level, e, into), move)
+        start()
+
+        def finish():
+            arrive()
+            unpack_rows(level, into)
+
+        return finish
+
+    def lanes(values):
+        return lax.broadcasted_iota(jnp.int32, values.shape, 1)
+
+    def z_low(values, step):
+        return jnp.where(lanes(values) < step, 0.0, pltpu.roll(values, step, 1))
+
+    def z_high(values, step):
+        return jnp.where(lanes(values) >= Z - step, 0.0, pltpu.roll(values, Z - step, 1))
+
+    def keep_inner(level, i, at, zl, zh):
+        step = 1 << level
+        inner_zl[level][i, at, :] = jnp.where(lanes(zl) < step, 0.0, zl)
+        inner_zh[level][i, at, :] = jnp.where(lanes(zh) >= Z - step, 0.0, zh)
+
+    grid_u, grid_v, grid_w, grid_r = grids
+    rows0 = Y0 + 2 * EDGE
+    win0 = pl.ds(PAD - EDGE, rows0)
+
+    def face(a, b):
+        return 2.0 / jnp.maximum(a + b, 0.5)
+
+    def faces(i, row=0, rows=rows0):
+        at, start = pl.ds(row, rows), row + PAD - EDGE
+        here = grid_r[i + 1, pl.ds(start, rows), :]
+        face_x[0][i, at, :] = face(grid_r[i, pl.ds(start, rows), :], here)
+        face_y[0][i, at, :] = face(grid_r[i + 1, pl.ds(start - 1, rows), :], here)
+        if row + rows == rows0:
+            last = PAD + EDGE + Y0
+            face_y[0][i, rows0 : rows0 + EDGE, :] = face(
+                grid_r[i + 1, last - 1 : last + EDGE - 1, :], grid_r[i + 1, last : last + EDGE, :]
+            )
+        zl, zh = face(z_low(here, 1), here), face(z_high(here, 1), here)
+        face_zl[0][i, at, :] = zl
+        face_zh[0][i, at, :] = zh
+        keep_inner(0, i, at, zl, zh)
+
+    def inside_rows(level, row, rows):
+        Y = dims(level)[1]
+        at = lax.broadcasted_iota(jnp.int32, (rows, Z), 0) + row
+        return jnp.logical_and(
+            jnp.logical_or(side_y[-1], at >= EDGE), jnp.logical_or(side_y[1], at < EDGE + Y)
+        )
+
+    def weigh(level, i, row=0, rows=None):
+        X, Y = dims(level)
+        h, rows = HALO[level], rows or Y + 2 * EDGE
+        at = pl.ds(row, rows)
+        total = face_x[level][i, at, :] + face_x[level][i + 1, at, :]
+        total += face_y[level][i, at, :] + face_y[level][i, pl.ds(row + 1, rows), :]
+        total += face_zl[level][i, at, :] + face_zh[level][i, at, :]
+        inside = jnp.logical_and(
+            jnp.logical_or(low[-1], i >= h), jnp.logical_or(low[1], i < h + X)
+        )
+        w = jnp.where(jnp.logical_and(inside_rows(level, row, rows), inside), DAMPING / total, 0.0)
+        diag[level][i, at, :] = total
+        weight[level][i, at, :] = w
+        return w
+
+    def first(j, row=0, rows=rows0):
+        at, start = pl.ds(row, rows), row + PAD - EDGE
+        mid = pl.ds(start, rows)
+        w = weigh(0, j + HALO[0] - HX[0], row, rows)
+        wz = grid_w[j + FIELD_HALO[2] - HX[0], mid, :]
+        u_at, v_at = j + FIELD_HALO[0] - HX[0], j + FIELD_HALO[1] - HX[0]
+        du = grid_u[u_at + 1, mid, :] - grid_u[u_at - 1, mid, :]
+        dv = grid_v[v_at, pl.ds(start + 1, rows), :] - grid_v[v_at, pl.ds(start - 1, rows), :]
+        b = -0.5 * ((du + dv) + (z_high(wz, 1) - z_low(wz, 1)))
+        source[0][j, at, :] = b
+        iterates[0][0, j, mid, :] = w * b
+
+    def planes_of(act, low_j, high_j, edges_only=False, unroll=2):
+        def one(j, carry):
+            if edges_only:
+                act(j, 0, PAD)
+                act(j, rows0 - PAD, PAD)
+            else:
+                act(j)
+            return carry
+
+        lax.fori_loop(low_j, high_j, one, 0, unroll=unroll)
+
+    n_faces, n_first = X0 + 2 * HALO[0], X0 + 2 * HX[0]
+    face_from, face_to = HALO[0] + 1, HALO[0] + X0 - 1
+    first_from, first_to = HX[0] + 1, HX[0] + X0 - 2
+    field_start, field_arrive = exchange(field_refs, 0)
+    field_start()
+    push()
+    planes_of(faces, face_from, face_to)
+    planes_of(first, first_from, first_to)
+    field_arrive()
 
     for n, (f, h, j) in enumerate(planes):
         for dx, x in ((-1, j), (1, h + X0 + j)):
@@ -450,82 +557,14 @@
                 )
                 keep_rows(end, x, uvw, r)
 
-    def lanes(values):
-        return lax.broadcasted_iota(jnp.int32, values.shape, 1)
-
-    def z_low(values, step):
-        return jnp.where(lanes(values) < step, 0.0, pltpu.roll(values, step, 1))
-
-    def z_high(values, step):
-        return jnp.where(lanes(values) >= Z - step, 0.0, pltpu.roll(values, Z - step, 1))
-
-    def keep_inner(level, i, zl, zh):
-        step = 1 << level
-        inner_zl[level][i] = jnp.where(lanes(zl) < step, 0.0, zl)
-        inner_zh[level][i] = jnp.where(lanes(zh) >= Z - step, 0.0, zh)
-
     push()
-    grid_u, grid_v, grid_w, grid_r = grids
-    rows0 = Y0 + 2 * EDGE
-    win0 = pl.ds(PAD - EDGE, rows0)
-
-    def face(a, b):
-        return 2.0 / jnp.maximum(a + b, 0.5)
-
-    def faces(i, carry):
-        here = grid_r[i + 1, win0, :]
-        face_x[0][i] = face(grid_r[i, win0, :], here)
-        face_y[0][i, :rows0, :] = face(grid_r[i + 1, pl.ds(PAD - EDGE - 1, rows0), :], here)
-        last = PAD + EDGE + Y0
-        face_y[0][i, rows0 : rows0 + EDGE, :] = face(
-            grid_r[i + 1, last - 1 : last + EDGE - 1, :], grid_r[i + 1, last : last + EDGE, :]
-        )
-        zl, zh = face(z_low(here, 1), here), face(z_high(here, 1), here)
-        face_zl[0][i] = zl
-        face_zh[0][i] = zh
-        keep_inner(0, i, zl, zh)
-        return carry
-
-    n_faces = X0 + 2 * HALO[0]
-    lax.fori_loop(0, n_faces, faces, 0, unroll=4)
+    planes_of(faces, 0, face_from)
+    planes_of(faces, face_to, n_faces)
+    planes_of(faces, face_from, face_to, edges_only=True)
     face_x[0][n_faces] = face(grid_r[n_faces, win0, :], grid_r[n_faces + 1, win0, :])
-
-    def inside_rows(level):
-        Y = dims(level)[1]
-        at = lax.broadcasted_iota(jnp.int32, (Y + 2 * EDGE, Z), 0)
-        return jnp.logical_and(
-            jnp.logical_or(side_y[-1], at >= EDGE), jnp.logical_or(side_y[1], at < EDGE + Y)
-        )
-
-    def weigh(level, i):
-        X, Y = dims(level)
-        h, rows = HALO[level], Y + 2 * EDGE
-        total = face_x[level][i] + face_x[level][i + 1]
-        total += face_y[level][i, :rows, :] + face_y[level][i, pl.ds(1, rows), :]
-        total += face_zl[level][i] + face_zh[level][i]
-        inside = jnp.logical_and(
-            jnp.logical_or(low[-1], i >= h), jnp.logical_or(low[1], i < h + X)
-        )
-        w = jnp.where(jnp.logical_and(inside_rows(level), inside), DAMPING / total, 0.0)
-        diag[level][i] = total
-        weight[level][i] = w
-        return w
-
-    def first(j, carry):
-        w = weigh(0, j + HALO[0] - HX)
-        wz = grid_w[j + FIELD_HALO[2] - HX, win0, :]
-        u_at, v_at = j + FIELD_HALO[0] - HX, j + FIELD_HALO[1] - HX
-        du = grid_u[u_at + 1, win0, :] - grid_u[u_at - 1, win0, :]
-        dv = (
-            grid_v[v_at, pl.ds(PAD - EDGE + 1, rows0), :]
-            - grid_v[v_at, pl.ds(PAD - EDGE - 1, rows0), :]
-        )
-        b = -0.5 * ((du + dv) + (z_high(wz, 1) - z_low(wz, 1)))
-        source[0][j] = b
-        iterates[0][0, j, win0, :] = w * b
-        return carry
-
-    lax.fori_loop(0, X0 + 2 * HX, first, 0, unroll=4)
+    planes_of(first, 0, first_from, unroll=3)
+    planes_of(first, first_to, n_first, unroll=4)
+    planes_of(first, first_from, first_to, edges_only=True)
 
     def z_bit(values, level):
         return (lanes(values) // (1 << level)) % 2 == 1
@@ -643,7 +682,7 @@
         edge = 0 if own else EDGE
         start, rows = PAD - edge, Y + 2 * edge
         at = pl.ds(EDGE - edge, rows)
-        i, j = x + HALO[level], x + HX
+        i, j = x + HALO[level], x + HX[level]
         here = p[e, j, pl.ds(start, rows), :]
         total = (
             face_x[level][i, at, :] * p[e, j - 1, pl.ds(start, rows), :]
@@ -664,25 +703,31 @@
         w = weight[level][x + HALO[level], pl.ds(EDGE - edge, Y + 2 * edge), :]
         if e == 0:
             return (1.0 + KEEP) * here + w * total
-        start = iterates[level][0, x + HX, pl.ds(PAD - edge, Y + 2 * edge), :]
+        start = iterates[level][0, x + HX[level], pl.ds(PAD - edge, Y + 2 * edge), :]
         return (KEEP * here + start) + w * total
 
-    def wide_sweep(level, e):
+    def wide_sweep(level, e, halo):
         X, Y = dims(level)
 
         def plane(j, carry):
-            iterates[level][e + 1, j + HX - 1, pl.ds(PAD - EDGE, Y + 2 * EDGE), :] = sweep(
-                level, e, j - 1, False
+            x = j - halo
+            iterates[level][e + 1, x + HX[level], pl.ds(PAD - EDGE, Y + 2 * EDGE), :] = sweep(
+                level, e, x, False
             )
             return carry
 
-        lax.fori_loop(0, X + 2, plane, 0, unroll=3 if level == 0 else 2)
-
+        lax.fori_loop(0, X + 2 * halo, plane, 0, unroll=3 if X + 2 * halo == 18 else 2)
+
+    finish_first = None
     for level in range(LEVELS):
         X, Y = dims(level)
         if level > 0:
-            level_exchange(level, 0, level)
-        wide_sweep(level, 0)
+            finish = level_exchange(level, 0, 0, level)
+            push()
+            finish()
+        wide_sweep(level, 0, 1)
+        if level == 0:
+            finish_first = level_exchange(0, 1, 2, LEVELS)
         h, half, last = HALO[level], Y // 2, level + 1 == LEVELS
         own_rows = pl.ds(EDGE, Y)
 
@@ -691,7 +736,7 @@
             for k in range(2):
                 fine = 2 * x + k
                 here, total = neighbour_sum(level, 1, fine, True)
-                b = source[0][fine + HX, own_rows, :] if level == 0 else source[level][fine]
+                b = source[0][fine + HX[0], own_rows, :] if level == 0 else source[level][fine]
                 left = (b - diag[level][fine + h, own_rows, :] * here) + total
                 both = left if both is None else both + left
             tmp[:Y, :] = both
@@ -704,7 +749,7 @@
             else:
                 source[level + 1][x] = summed
                 w = weight[level + 1][x + HALO[level + 1], pl.ds(EDGE, half), :]
-                iterates[level + 1][0, x + HX, pl.ds(PAD, half), :] = w * summed
+                iterates[level + 1][0, x + HX[level + 1], pl.ds(PAD, half), :] = w * summed
             return carry
 
         if last:
@@ -753,31 +798,61 @@
     for x in range(X):
         answer[LEVELS][x] = coef[7, narrow * X + x]
 
-    for level in reversed(range(LEVELS)):
+    def repeat_rows(e, count):
+        tmp[pl.ds(0, count, stride=2), :] = e
+        tmp[pl.ds(1, count, stride=2), :] = e
+        return tmp[: 2 * count, :]
+
+    for level in reversed(range(1, LEVELS)):
         X, Y = dims(level)
         half = Y // 2
 
         def raised(x, carry, level=level, Y=Y, half=half):
-            e = answer[level + 1][x // 2]
-            tmp[pl.ds(0, half, stride=2), :] = e
-            tmp[pl.ds(1, half, stride=2), :] = e
-            iterates[level][2, x + HX, PAD : PAD + Y, :] = (
-                iterates[level][1, x + HX, PAD : PAD + Y, :] + tmp[:Y, :]
+            e = repeat_rows(answer[level + 1][x // 2], half)
+            at = x + HX[level]
+            iterates[level][2, at, PAD : PAD + Y, :] = (
+                iterates[level][1, at, PAD : PAD + Y, :] + e
             )
             return carry
 
         lax.fori_loop(0, X, raised, 0, unroll=4)
-        level_exchange(level, 2, LEVELS + level)
-        wide_sweep(level, 2)
-        result = pressure if level == 0 else answer[level]
-
-        def close(x, carry, level=level, result=result):
-            result[x] = sweep(level, 3, x, True)
+        finish = level_exchange(level, 2, 2, LEVELS + level)
+        push()
+        finish()
+        out_halo = 1 if level == 1 else 0
+        wide_sweep(level, 2, 1 + out_halo)
+
+        def close(j, carry, level=level, out_halo=out_halo):
+            if out_halo:
+                near_answer[j, pl.ds(PAD - EDGE, dims(level)[1] + 2 * EDGE), :] = sweep(
+                    level, 3, j - out_halo, False
+                )
+            else:
+                answer[level][j] = sweep(level, 3, j, True)
             return carry
 
-        lax.fori_loop(0, X, close, 0, unroll=4)
-
-    assert len(pushed) == len(SHARES)
+        lax.fori_loop(0, X + 2 * out_halo, close, 0, unroll=2)
+
+    for x in range(X0):
+        iterates[0][2, x + HX[0], PAD : PAD + Y0, :] = iterates[0][1, x + HX[0], PAD : PAD + Y0, :]
+    finish_first()
+    coarse_rows = pl.ds(PAD - EDGE // 2, Y0 // 2 + EDGE)
+
+    def raise_first(j, carry):
+        e = repeat_rows(near_answer[j // 2, coarse_rows, :], Y0 // 2 + EDGE)
+        iterates[0][2, j, win0, :] = iterates[0][2, j, win0, :] + e
+        return carry
+
+    lax.fori_loop(0, X0 + 2 * HX[0], raise_first, 0, unroll=4)
+    wide_sweep(0, 2, 1)
+
+    def close_first(x, carry):
+        pressure[x] = sweep(0, 3, x, True)
+        return carry
+
+    lax.fori_loop(0, X0, close_first, 0, unroll=4)
+
+    assert len(pushed) == len(SHARES) + 1
     pressure_copy = pltpu.make_async_copy(pressure, pressure_ref, local_sem.at[4])
     pressure_copy.start()
 
@@ -856,7 +931,7 @@
         pltpu.SMEM((CAPACITY, owners, Z), jnp.int32),
         pltpu.SMEM((per_owner, Z), jnp.int32),
         f32(64, Z),
-        f32(Y0, Z),
+        f32(Y0 + 2 * PAD, Z),
         [f32(X0 + 2 * h, Y0 + 2 * PAD, Z) for h in FIELD_HALO],
         bf16(2, HALO_PLANES, Y0, Z),
         bf16(2, HALO_PLANES, Y0, Z),
@@ -864,9 +939,9 @@
         bf16(2, 2 * X0, PAD, Z),
         bf16(4, 2 * CORNER, PAD, Z),
         bf16(4, 2 * CORNER, PAD, Z),
-        [f32(4, X + 2 * HX, Y + 2 * PAD, Z) for l, X, Y in levels],
-        [f32(2, 2, X // 4, PAD, Z) for l, X, Y in levels],
-        [f32(2, 2, X // 4, PAD, Z) for l, X, Y in levels],
+        [f32(4, X + 2 * HX[l], Y + 2 * PAD, Z) for l, X, Y in levels],
+        [f32(2, 2, X * ROWS[l] // PAD, PAD, Z) for l, X, Y in levels],
+        [f32(2, 2, X * ROWS[l] // PAD, PAD, Z) for l, X, Y in levels],
         [f32(X + 2 * HALO[l] + 1, Y + 2 * EDGE, Z) for l, X, Y in levels],
         [f32(X + 2 * HALO[l], Y + 2 * EDGE + 8, Z) for l, X, Y in levels],
         faces,
@@ -875,8 +950,9 @@
         faces,
         faces,
         faces,
-        [f32(X0 + 2 * HX, Y0 + 2 * EDGE, Z)] + [f32(X, Y, Z) for l, X, Y in levels[1:]],
+        [f32(X0 + 2 * HX[0], Y0 + 2 * EDGE, Z)] + [f32(X, Y, Z) for l, X, Y in levels[1:]],
         [f32(*dims(level), Z) for level in range(LEVELS + 1)],
+        f32(dims(1)[0] + 2, dims(1)[1] + 2 * PAD, Z),
         f32(n_narrow, 5 * X3 + 1, Y3, Z),
         f32(n_narrow, X3, Y3, Z),
         f32(8, n_narrow * X3, Y3, Z),
@@ -902,7 +978,7 @@
         out_specs=(anywhere, anywhere),
         scratch_shapes=scratch,
         compiler_params=pltpu.CompilerParams(
-            collective_id=0, has_side_effects=True, vmem_limit_bytes=VMEM_LIMIT
+            collective_id=0, has_side_effects=True, vmem_limit_bytes=min(60, 46 + owners // 8) * 1024 * 1024
         ),
         cost_estimate=pl.CostEstimate(
             flops=200_000_000, bytes_accessed=200_000_000, transcendentals=0
@@ -910,8 +986,33 @@
     )(table, fields)
 
 
+def hand_over_kernel(migrated_ref, pressure_ref, migrated_out, pressure_out, sem):
+    copies = []
+    for n, (src, dst) in enumerate(((migrated_ref, migrated_out), (pressure_ref, pressure_out))):
+        size = src.shape[0] // PIECES
+        for g in range(PIECES):
+            piece = pl.ds(g * size, size)
+            copies.append(pltpu.make_async_copy(src.at[piece], dst.at[piece], sem.at[n, g]))
+    for copy in copies:
+        copy.start()
+    for copy in copies:
+        copy.wait()
+
+
+def hand_over(migrated, pressure):
+    anywhere = pl.BlockSpec(memory_space=pl.ANY)
+    return pl.pallas_call(
+        hand_over_kernel,
+        out_shape=tuple(jax.ShapeDtypeStruct(a.shape, a.dtype) for a in (migrated, pressure)),
+        in_specs=[anywhere, anywhere],
+        out_specs=(anywhere, anywhere),
+        scratch_shapes=[pltpu.SemaphoreType.DMA((2, PIECES))],
+        compiler_params=pltpu.CompilerParams(vmem_limit_bytes=1024 * 1024),
+    )(migrated, pressure)
+
+
 def shards(n_wide, n_narrow, target_slot, fields):
-    return call_solve(n_wide, n_narrow, target_slot.reshape(-1, Z), fields)
+    return hand_over(*call_solve(n_wide, n_narrow, target_slot.reshape(-1, Z), fields))
 
 
 def solution(mesh):

time: 126 us -> 122 us (0.968)
  the two profiles are of different devices: /device:TPU:0 before, /device:TPU:13 now
where the time goes in v2:
time: 122 us
  Pallas kernels  120 us (98%)
    pallas_call x1, Pallas kernels, call_solve(): pl.pallas_call(functools.partial(solve_kernel, n_wide, n_narrow), out_sha...  119 us

profile of v2, /device:TPU:13, one launch (start us, length us, event | category | flops | bytes accessed | tf_op | source)
XLA Modules:
  0.0 121.8 jit_solution(7605741889076552834)
XLA Ops:
  0.6 0.0 copy-start
  0.6 0.7 copy-done
  1.3 118.9 %shard_map.41 = (bf16[32,8,4096]{2,1,0:T(8,128)(2,1)S(1)}, f32[16,64,128]{2,1,0:T(8,128)S(1)}) custom-call(s32[8,128]{1,0:T(8,128)S(1)} %bitcast.1, bf16[32,8,4096]{2,1,0:T(8,128)(2,1)} %fields_ref.1), custom_call_target="tpu_custom_call" | custom-call | flops 200000000 | bytes 200000000 | tf_op jit(solution)/shard_map/pallas_call | solution.py:971
  120.2 1.6 %shard_map.42 = (bf16[32,8,4096]{2,1,0:T(8,128)(2,1)}, f32[16,64,128]{2,1,0:T(8,128)}) custom-call(bf16[32,8,4096]{2,1,0:T(8,128)(2,1)S(1)} %get-tuple-element.4.migrated_ref, f32[16,64,128]{2,1,0:T(8,128)S(1)} %get-tuple-element.5.pressure_ref), custom_call_target="tpu_custom_call" | custom-call | tf_op jit(solution)/shard_map/pallas_call | solution.py:1004
Async XLA Ops:
  0.6 0.7 copy-start

commit v3 on v2

--- a/solution.py
+++ b/solution.py
@@ -30,7 +30,8 @@
 HALO_PLANES = sum(FIELD_HALO)
 CORNER = max(FIELD_HALO)
 MESH = pl.DeviceIdType.MESH
-SHARES = (1, 1, 2, 1, 1, 1, 1, 1, 7)
+FAR = (4, 0, 1, 2, 1, 1, 1, 1, 1, 4)
+NEAR = (10, 0, 0, 0, 1, 1, 1, 1, 1, 0)
 OUT_GROUP = 8
 PIECES = 8
 SIDES = tuple((dx, dy) for dx in (-1, 0, 1) for dy in (-1, 0, 1) if dx or dy)
@@ -218,22 +219,24 @@
     lax.fori_loop(1, owners, pack_carried, 0)
 
     half_way = owners // 2
-    bounds = [1] + [
-        half_way + half_way * sum(SHARES[:k]) // sum(SHARES) for k in range(len(SHARES) + 1)
-    ]
+
+    def cuts(shares, first, end):
+        return [first + (end - first) * sum(shares[:k]) // sum(shares) for k in range(len(shares) + 1)]
+
+    far = cuts(FAR, half_way, owners)
+    near = cuts(NEAR, 1, half_way)
     pushed = []
+
+    def begin(k, carry):
+        carried_bulk(k).start()
+        return carry
 
     def push():
         turn_now = len(pushed)
         pushed.append(turn_now)
-        if bounds[turn_now] == bounds[turn_now + 1]:
-            return
-
-        def begin(k, carry):
-            carried_bulk(k).start()
-            return carry
-
-        lax.fori_loop(bounds[turn_now], bounds[turn_now + 1], begin, 0)
+        for bounds in (far, near):
+            if bounds[turn_now] < bounds[turn_now + 1]:
+                lax.fori_loop(bounds[turn_now], bounds[turn_now + 1], begin, 0)
 
     push()
     for level in range(LEVELS):
@@ -538,6 +541,12 @@
     field_start, field_arrive = exchange(field_refs, 0)
     field_start()
     push()
+
+    def solved_end(k, carry):
+        solved_bulk(k).wait_send()
+        return carry
+
+    lax.fori_loop(1, owners, solved_end, 0, unroll=False)
     planes_of(faces, face_from, face_to)
     planes_of(first, first_from, first_to)
     field_arrive()
@@ -852,7 +861,7 @@
 
     lax.fori_loop(0, X0, close_first, 0, unroll=4)
 
-    assert len(pushed) == len(SHARES) + 1
+    assert len(pushed) == len(FAR)
     pressure_copy = pltpu.make_async_copy(pressure, pressure_ref, local_sem.at[4])
     pressure_copy.start()
 
@@ -861,37 +870,32 @@
         return carry
 
     lax.fori_loop(0, PER_OWNER, merge_solved, 0, unroll=4)
-
-    def carried_arrive(k, carry):
-        carried_bulk(k, incoming=True).wait_recv()
-        return carry
-
-    lax.fori_loop(1, owners, carried_arrive, 0)
-
-    def out_copy(g):
-        group = pl.ds(g * OUT_GROUP, OUT_GROUP)
-        return pltpu.make_async_copy(merged.at[group], migrated_ref.at[group], out_sem.at[g])
-
-    for g in range(PER_OWNER // OUT_GROUP):
-
-        def merge_carried(q, carry):
-            merged[q, SOLVED:] = moved[receive_index[q, 0]]
-            return carry
-
-        lax.fori_loop(g * OUT_GROUP, (g + 1) * OUT_GROUP, merge_carried, 0, unroll=4)
-        out_copy(g).start()
-
-    def end(k, carry):
-        carried_bulk(k).wait_send()
-        solved_bulk(k).wait_send()
-        return carry
-
-    lax.fori_loop(1, owners, end, 0)
     face_drain()
     source_drain()
     for drain in drains:
         drain()
     pressure_copy.wait()
+
+    def carried_end(k, carry):
+        carried_bulk(k).wait_send()
+        carried_bulk(k, incoming=True).wait_recv()
+        return carry
+
+    lax.fori_loop(1, owners, carried_end, 0)
+
+    def out_copy(g):
+        group = pl.ds(g * OUT_GROUP, OUT_GROUP)
+        return pltpu.make_async_copy(merged.at[group], migrated_ref.at[group], out_sem.at[g])
+
+    for g in range(PER_OWNER // OUT_GROUP):
+
+        def merge_carried(q, carry):
+            merged[q, SOLVED:] = moved[receive_index[q, 0]]
+            return carry
+
+        lax.fori_loop(g * OUT_GROUP, (g + 1) * OUT_GROUP, merge_carried, 0, unroll=4)
+        out_copy(g).start()
+
     for g in range(PER_OWNER // OUT_GROUP):
         out_copy(g).wait()
 

time: 122 us -> 118 us (0.967)
  the two profiles are of different devices: /device:TPU:13 before, /device:TPU:0 now
where the time goes in v3:
time: 118 us; the launch traced here: 116 us
  Pallas kernels  114 us (97%)
    pallas_call x1, Pallas kernels, call_solve(): pl.pallas_call(functools.partial(solve_kernel, n_wide, n_narrow), out_sha...  113 us

profile of v3, /device:TPU:0, one launch (start us, length us, event | category | flops | bytes accessed | tf_op | source)
XLA Modules:
  0.0 115.8 jit_solution(4828313143199783403)
XLA Ops:
  0.6 0.0 copy-start
  0.6 0.7 copy-done
  1.3 112.8 %shard_map.41 = (bf16[32,8,4096]{2,1,0:T(8,128)(2,1)S(1)}, f32[16,64,128]{2,1,0:T(8,128)S(1)}) custom-call(s32[8,128]{1,0:T(8,128)S(1)} %bitcast.1, bf16[32,8,4096]{2,1,0:T(8,128)(2,1)} %fields_ref.1), custom_call_target="tpu_custom_call" | custom-call | flops 200000000 | bytes 200000000 | tf_op jit(solution)/shard_map/pallas_call | solution.py:975
  114.2 1.6 %shard_map.42 = (bf16[32,8,4096]{2,1,0:T(8,128)(2,1)}, f32[16,64,128]{2,1,0:T(8,128)}) custom-call(bf16[32,8,4096]{2,1,0:T(8,128)(2,1)S(1)} %get-tuple-element.4.migrated_ref, f32[16,64,128]{2,1,0:T(8,128)S(1)} %get-tuple-element.5.pressure_ref), custom_call_target="tpu_custom_call" | custom-call | tf_op jit(solution)/shard_map/pallas_call | solution.py:1008
Async XLA Ops:
  0.6 0.7 copy-start

commit v4 on v3

--- a/solution.py
+++ b/solution.py
@@ -30,8 +30,8 @@
 HALO_PLANES = sum(FIELD_HALO)
 CORNER = max(FIELD_HALO)
 MESH = pl.DeviceIdType.MESH
-FAR = (4, 0, 1, 2, 1, 1, 1, 1, 1, 4)
-NEAR = (10, 0, 0, 0, 1, 1, 1, 1, 1, 0)
+FAR = (5, 0, 1, 2, 1, 1, 1, 1, 1, 3)
+NEAR = (9, 0, 0, 1, 1, 1, 1, 1, 1, 0)
 OUT_GROUP = 8
 PIECES = 8
 SIDES = tuple((dx, dy) for dx in (-1, 0, 1) for dy in (-1, 0, 1) if dx or dy)
@@ -234,7 +234,7 @@
     def push():
         turn_now = len(pushed)
         pushed.append(turn_now)
-        for bounds in (far, near):
+        for bounds in (near, far):
             if bounds[turn_now] < bounds[turn_now + 1]:
                 lax.fori_loop(bounds[turn_now], bounds[turn_now + 1], begin, 0)
 

time: 118 us -> 116 us (0.983)
  no operation moved by 1% of the time
where the time goes in v4:
time: 116 us; the launch traced here: 115 us
  Pallas kernels  113 us (97%)
    pallas_call x1, Pallas kernels, call_solve(): pl.pallas_call(functools.partial(solve_kernel, n_wide, n_narrow), out_sha...  112 us

profile of v4, /device:TPU:0, one launch (start us, length us, event | category | flops | bytes accessed | tf_op | source)
XLA Modules:
  0.0 114.8 jit_solution(7501268839648062502)
XLA Ops:
  0.6 0.0 copy-start
  0.6 0.7 copy-done
  1.3 111.8 %shard_map.41 = (bf16[32,8,4096]{2,1,0:T(8,128)(2,1)S(1)}, f32[16,64,128]{2,1,0:T(8,128)S(1)}) custom-call(s32[8,128]{1,0:T(8,128)S(1)} %bitcast.1, bf16[32,8,4096]{2,1,0:T(8,128)(2,1)} %fields_ref.1), custom_call_target="tpu_custom_call" | custom-call | flops 200000000 | bytes 200000000 | tf_op jit(solution)/shard_map/pallas_call | solution.py:975
  113.2 1.6 %shard_map.42 = (bf16[32,8,4096]{2,1,0:T(8,128)(2,1)}, f32[16,64,128]{2,1,0:T(8,128)}) custom-call(bf16[32,8,4096]{2,1,0:T(8,128)(2,1)S(1)} %get-tuple-element.4.migrated_ref, f32[16,64,128]{2,1,0:T(8,128)S(1)} %get-tuple-element.5.pressure_ref), custom_call_target="tpu_custom_call" | custom-call | tf_op jit(solution)/shard_map/pallas_call | solution.py:1008
Async XLA Ops:
  0.6 0.7 copy-start

commit v5 on v4

--- a/solution.py
+++ b/solution.py
@@ -32,7 +32,6 @@
 MESH = pl.DeviceIdType.MESH
 FAR = (5, 0, 1, 2, 1, 1, 1, 1, 1, 3)
 NEAR = (9, 0, 0, 1, 1, 1, 1, 1, 1, 0)
-OUT_GROUP = 8
 PIECES = 8
 SIDES = tuple((dx, dy) for dx in (-1, 0, 1) for dy in (-1, 0, 1) if dx or dy)
 
@@ -46,16 +45,14 @@
     n_narrow,
     target_ref,
     fields_ref,
-    migrated_ref,
-    pressure_ref,
+    merged,
+    pressure,
     target,
     fields,
     solved,
     carried,
     arrived,
     moved,
-    merged,
-    pressure,
     send_index_v,
     receive_index_v,
     send_index,
@@ -95,7 +92,6 @@
     solved_send_sem,
     solved_recv_sem,
     local_sem,
-    out_sem,
 ):
     wide = lax.axis_index("wide")
     narrow = lax.axis_index("narrow")
@@ -862,8 +858,6 @@
     lax.fori_loop(0, X0, close_first, 0, unroll=4)
 
     assert len(pushed) == len(FAR)
-    pressure_copy = pltpu.make_async_copy(pressure, pressure_ref, local_sem.at[4])
-    pressure_copy.start()
 
     def merge_solved(q, carry):
         merged[q, :SOLVED] = arrived[receive_index[q, 0]]
@@ -874,7 +868,6 @@
     source_drain()
     for drain in drains:
         drain()
-    pressure_copy.wait()
 
     def carried_end(k, carry):
         carried_bulk(k).wait_send()
@@ -883,21 +876,11 @@
 
     lax.fori_loop(1, owners, carried_end, 0)
 
-    def out_copy(g):
-        group = pl.ds(g * OUT_GROUP, OUT_GROUP)
-        return pltpu.make_async_copy(merged.at[group], migrated_ref.at[group], out_sem.at[g])
-
-    for g in range(PER_OWNER // OUT_GROUP):
-
-        def merge_carried(q, carry):
-            merged[q, SOLVED:] = moved[receive_index[q, 0]]
-            return carry
-
-        lax.fori_loop(g * OUT_GROUP, (g + 1) * OUT_GROUP, merge_carried, 0, unroll=4)
-        out_copy(g).start()
-
-    for g in range(PER_OWNER // OUT_GROUP):
-        out_copy(g).wait()
+    def merge_carried(q, carry):
+        merged[q, SOLVED:] = moved[receive_index[q, 0]]
+        return carry
+
+    lax.fori_loop(0, PER_OWNER, merge_carried, 0, unroll=8)
 
 
 def f32(*shape):
@@ -928,8 +911,6 @@
         packs["carried"],
         packs["solved"],
         packs["carried"],
-        bf16(*fields.shape),
-        f32(X0, Y0, Z),
         pltpu.VMEM((CAPACITY, owners, Z), jnp.int32),
         pltpu.VMEM((per_owner, Z), jnp.int32),
         pltpu.SMEM((CAPACITY, owners, Z), jnp.int32),
@@ -968,8 +949,7 @@
         dma((owners,)),
         dma((owners,)),
         dma((owners,)),
-        dma((5,)),
-        dma((per_owner // OUT_GROUP,)),
+        dma((4,)),
     ]
     anywhere = pl.BlockSpec(memory_space=pl.ANY)
     return pl.pallas_call(
@@ -979,7 +959,7 @@
             jax.ShapeDtypeStruct((X0, Y0, Z), jnp.float32),
         ),
         in_specs=[anywhere, anywhere],
-        out_specs=(anywhere, anywhere),
+        out_specs=(pl.BlockSpec(memory_space=pltpu.VMEM),) * 2,
         scratch_shapes=scratch,
         compiler_params=pltpu.CompilerParams(
             collective_id=0, has_side_effects=True, vmem_limit_bytes=min(60, 46 + owners // 8) * 1024 * 1024

time: 116 us -> 115 us (level)
  no operation moved by 1% of the time
where the time goes in v5:
time: 115 us; the launch traced here: 114 us
  Pallas kernels  113 us (98%)
    pallas_call x1, Pallas kernels, call_solve(): pl.pallas_call(functools.partial(solve_kernel, n_wide, n_narrow), out_sha...  112 us

profile of v5, /device:TPU:0, one launch (start us, length us, event | category | flops | bytes accessed | tf_op | source)
XLA Modules:
  0.0 114.5 jit_solution(17075923247840779454)
XLA Ops:
  0.6 0.0 copy-start
  0.6 0.7 copy-done
  1.3 111.5 %shard_map.41 = (bf16[32,8,4096]{2,1,0:T(8,128)(2,1)S(1)}, f32[16,64,128]{2,1,0:T(8,128)S(1)}) custom-call(s32[8,128]{1,0:T(8,128)S(1)} %bitcast.1, bf16[32,8,4096]{2,1,0:T(8,128)(2,1)} %fields_ref.1), custom_call_target="tpu_custom_call" | custom-call | flops 200000000 | bytes 200000000 | tf_op jit(solution)/shard_map/pallas_call | solution.py:955
  112.9 1.6 %shard_map.42 = (bf16[32,8,4096]{2,1,0:T(8,128)(2,1)}, f32[16,64,128]{2,1,0:T(8,128)}) custom-call(bf16[32,8,4096]{2,1,0:T(8,128)(2,1)S(1)} %get-tuple-element.4.migrated_ref, f32[16,64,128]{2,1,0:T(8,128)S(1)} %get-tuple-element.5.pressure_ref), custom_call_target="tpu_custom_call" | custom-call | tf_op jit(solution)/shard_map/pallas_call | solution.py:988
Async XLA Ops:
  0.6 0.7 copy-start

commit v6 on v5

--- a/solution.py
+++ b/solution.py
@@ -153,6 +153,47 @@
     index_copy = pltpu.make_async_copy(send_index_v, send_index, local_sem.at[2])
     index_copy.start()
 
+    index_copy.wait()
+    fields_copy.wait()
+    pl.semaphore_wait(barrier, owners - 1)
+
+    def block(owner):
+        return pl.ds(owner * CAPACITY, CAPACITY)
+
+    def bulk(whom, packed, landed, send, recv, k, incoming=False):
+        owner, device = whom(k)
+        return pltpu.make_async_remote_copy(
+            src_ref=packed.at[block(me if incoming else owner)],
+            dst_ref=landed.at[block(owner if incoming else me)],
+            send_sem=send.at[k],
+            recv_sem=recv.at[k],
+            device_id=device,
+            device_id_type=MESH,
+        )
+
+    solved_bulk = functools.partial(bulk, partner, solved, arrived, solved_send_sem, solved_recv_sem)
+    carried_bulk = functools.partial(bulk, at_distance, carried, moved, carry_send_sem, carry_recv_sem)
+
+    def pack_solved(k, carry):
+        owner, _ = partner(k)
+        for r in range(CAPACITY):
+            solved[owner * CAPACITY + r] = fields[send_index[r, owner, 0], :SOLVED]
+        solved_bulk(k).start()
+        return carry
+
+    def pack_carried(k, carry):
+        owner, _ = at_distance(k)
+        for r in range(CAPACITY):
+            carried[owner * CAPACITY + r] = fields[send_index[r, owner, 0], SOLVED:]
+        return carry
+
+    lax.fori_loop(1, owners, pack_solved, 0)
+    for r in range(CAPACITY):
+        patch = fields[send_index[r, me, 0]]
+        arrived[me * CAPACITY + r] = patch[:SOLVED]
+        moved[me * CAPACITY + r] = patch[SOLVED:]
+    lax.fori_loop(1, owners, pack_carried, 0)
+
     table = target[...]
     t_rows = table.shape[0]
     t_lane = lax.broadcasted_iota(jnp.int32, (t_rows, Z), 1)
@@ -172,47 +213,6 @@
     receive_index_v[...] = jnp.broadcast_to(slots_q, (PER_OWNER, Z))
     receive_copy = pltpu.make_async_copy(receive_index_v, receive_index, local_sem.at[3])
     receive_copy.start()
-
-    index_copy.wait()
-    fields_copy.wait()
-    pl.semaphore_wait(barrier, owners - 1)
-
-    def block(owner):
-        return pl.ds(owner * CAPACITY, CAPACITY)
-
-    def bulk(whom, packed, landed, send, recv, k, incoming=False):
-        owner, device = whom(k)
-        return pltpu.make_async_remote_copy(
-            src_ref=packed.at[block(me if incoming else owner)],
-            dst_ref=landed.at[block(owner if incoming else me)],
-            send_sem=send.at[k],
-            recv_sem=recv.at[k],
-            device_id=device,
-            device_id_type=MESH,
-        )
-
-    solved_bulk = functools.partial(bulk, partner, solved, arrived, solved_send_sem, solved_recv_sem)
-    carried_bulk = functools.partial(bulk, at_distance, carried, moved, carry_send_sem, carry_recv_sem)
-
-    def pack_solved(k, carry):
-        owner, _ = partner(k)
-        for r in range(CAPACITY):
-            solved[owner * CAPACITY + r] = fields[send_index[r, owner, 0], :SOLVED]
-        solved_bulk(k).start()
-        return carry
-
-    def pack_carried(k, carry):
-        owner, _ = at_distance(k)
-        for r in range(CAPACITY):
-            carried[owner * CAPACITY + r] = fields[send_index[r, owner, 0], SOLVED:]
-        return carry
-
-    lax.fori_loop(1, owners, pack_solved, 0)
-    for r in range(CAPACITY):
-        patch = fields[send_index[r, me, 0]]
-        arrived[me * CAPACITY + r] = patch[:SOLVED]
-        moved[me * CAPACITY + r] = patch[SOLVED:]
-    lax.fori_loop(1, owners, pack_carried, 0)
 
     half_way = owners // 2
 

time: 115 us -> 115 us (level)
  no operation moved by 1% of the time
where the time goes in v6:
time: 115 us
  Pallas kernels  114 us (99%)
    pallas_call x1, Pallas kernels, call_solve(): pl.pallas_call(functools.partial(solve_kernel, n_wide, n_narrow), out_sha...  112 us

profile of v6, /device:TPU:0, one launch (start us, length us, event | category | flops | bytes accessed | tf_op | source)
XLA Modules:
  0.0 114.8 jit_solution(11876834513598193507)
XLA Ops:
  0.6 0.0 copy-start
  0.6 0.7 copy-done
  1.3 111.9 %shard_map.41 = (bf16[32,8,4096]{2,1,0:T(8,128)(2,1)S(1)}, f32[16,64,128]{2,1,0:T(8,128)S(1)}) custom-call(s32[8,128]{1,0:T(8,128)S(1)} %bitcast.1, bf16[32,8,4096]{2,1,0:T(8,128)(2,1)} %fields_ref.1), custom_call_target="tpu_custom_call" | custom-call | flops 200000000 | bytes 200000000 | tf_op jit(solution)/shard_map/pallas_call | solution.py:955
  113.2 1.6 %shard_map.42 = (bf16[32,8,4096]{2,1,0:T(8,128)(2,1)}, f32[16,64,128]{2,1,0:T(8,128)}) custom-call(bf16[32,8,4096]{2,1,0:T(8,128)(2,1)S(1)} %get-tuple-element.4.migrated_ref, f32[16,64,128]{2,1,0:T(8,128)S(1)} %get-tuple-element.5.pressure_ref), custom_call_target="tpu_custom_call" | custom-call | tf_op jit(solution)/shard_map/pallas_call | solution.py:988
Async XLA Ops:
  0.6 0.7 copy-start

commit v7 on v5

--- a/solution.py
+++ b/solution.py
@@ -31,7 +31,7 @@
 CORNER = max(FIELD_HALO)
 MESH = pl.DeviceIdType.MESH
 FAR = (5, 0, 1, 2, 1, 1, 1, 1, 1, 3)
-NEAR = (9, 0, 0, 1, 1, 1, 1, 1, 1, 0)
+NEAR = (9, 0, 1, 0, 1, 1, 1, 1, 1, 0)
 PIECES = 8
 SIDES = tuple((dx, dy) for dx in (-1, 0, 1) for dy in (-1, 0, 1) if dx or dy)
 

time: 115 us -> 115 us (level)
  no operation moved by 1% of the time
where the time goes in v7:
time: 115 us
  Pallas kernels  113 us (98%)
    pallas_call x1, Pallas kernels, call_solve(): pl.pallas_call(functools.partial(solve_kernel, n_wide, n_narrow), out_sha...  112 us

profile of v7, /device:TPU:0, one launch (start us, length us, event | category | flops | bytes accessed | tf_op | source)
XLA Modules:
  0.0 114.7 jit_solution(14123042453191374580)
XLA Ops:
  0.6 0.0 copy-start
  0.6 0.7 copy-done
  1.3 111.8 %shard_map.41 = (bf16[32,8,4096]{2,1,0:T(8,128)(2,1)S(1)}, f32[16,64,128]{2,1,0:T(8,128)S(1)}) custom-call(s32[8,128]{1,0:T(8,128)S(1)} %bitcast.1, bf16[32,8,4096]{2,1,0:T(8,128)(2,1)} %fields_ref.1), custom_call_target="tpu_custom_call" | custom-call | flops 200000000 | bytes 200000000 | tf_op jit(solution)/shard_map/pallas_call | solution.py:955
  113.1 1.6 %shard_map.42 = (bf16[32,8,4096]{2,1,0:T(8,128)(2,1)}, f32[16,64,128]{2,1,0:T(8,128)}) custom-call(bf16[32,8,4096]{2,1,0:T(8,128)(2,1)S(1)} %get-tuple-element.4.migrated_ref, f32[16,64,128]{2,1,0:T(8,128)S(1)} %get-tuple-element.5.pressure_ref), custom_call_target="tpu_custom_call" | custom-call | tf_op jit(solution)/shard_map/pallas_call | solution.py:988
Async XLA Ops:
  0.6 0.7 copy-start
